TPU v7x, 256 devices: a whole 4x4x8 slice. The times are simulated.
256 devices in a mesh: lon: 32 (over z, y_hi, core), lat: 8 (over y_lo, x).
Axes of the slice: x: 4, y: 4 (y_hi: 2, y_lo: 2; y = y_hi * 2 + y_lo), z: 8, core: 2. Of those that a mesh axis runs over, the one named last changes fastest.
Arguments:
- features: bfloat16 [65536, 512], P(('lon', 'lat')), may hold values from -6 to 6
- cotangent: bfloat16 [65536, 512], P(('lon', 'lat')), may hold values from -6 to 6
- w_query: bfloat16 [512, 512], replicated, may hold values from -0.3 to 0.3
- w_key: bfloat16 [512, 512], replicated, may hold values from -0.3 to 0.3
- w_value: bfloat16 [512, 512], replicated, may hold values from -0.25 to 0.25
- neighbour: int32 [65536, 16], P(('lon', 'lat')), may hold values from 0 to 767, as said below
- slot_mask: int32 [65536, 16], P(('lon', 'lat')), may hold values 0 or 1
- send_rows: int32 [1024, 128], P(('lon', 'lat')), may hold values from 0 to 255
Outputs:
- features_grad: bfloat16 [65536, 512], P(('lon', 'lat'))
- weight_grads: float32 [1536, 512], P(('lon', 'lat'))
Inputs may be any that keep to these rules, and one draw needn't show every extreme that they name: `neighbour`: the 16 slots of a node name 16 different rows of its sector's table.
All inputs are finite; a program needn't handle non-finite values. No bound on the sum of `slot_mask` on one device may be relied on, other than what follows from the above.
Results may differ from a plain program's by a relative error of at most 0.02.
Values may be sent and summed in bfloat16 or wider, within the bound.
A program may use at most 128 MiB of HBM per device.

v0:
```python
import jax
import jax.numpy as jnp
from jax import lax
from jax.sharding import PartitionSpec as P

HEADS = 4


def extended(cells, sides, width, closed):
    for axis, dim in sides:
        count = lax.axis_size(axis)
        ends = count if closed else count - 1
        head = lax.slice_in_dim(cells, 0, width, axis=dim)
        tail = lax.slice_in_dim(cells, cells.shape[dim] - width, cells.shape[dim], axis=dim)
        cells = jnp.concatenate(
            [
                lax.ppermute(tail, axis, [(i, (i + 1) % count) for i in range(ends)]),
                cells,
                lax.ppermute(head, axis, [((i + 1) % count, i) for i in range(ends)]),
            ],
            axis=dim,
        )
    return cells


def attend_back(queries, grad_out, gathered, usable):
    row_count, slot_count = usable.shape
    model_width = queries.shape[1]
    head_size = model_width // HEADS
    score_scale = head_size ** (-0.5)
    query_heads = queries.reshape(row_count, HEADS, head_size)
    grad_heads = grad_out.reshape(row_count, HEADS, head_size)
    key_heads = gathered[:, :, :model_width].reshape(row_count, slot_count, HEADS, head_size)
    value_heads = gathered[:, :, model_width:].reshape(row_count, slot_count, HEADS, head_size)
    scores = (
        jnp.einsum("rhd,rshd->rsh", query_heads, key_heads, preferred_element_type=jnp.float32)
        * score_scale
    )
    allowed = usable[:, :, None] > 0
    masked = jnp.where(allowed, scores, -1e30)
    largest = jnp.max(masked, axis=1, keepdims=True)
    expvals = jnp.where(allowed, jnp.exp(masked - largest), 0.0)
    probability = expvals / jnp.sum(expvals, axis=1, keepdims=True)
    rounded = probability.astype(jnp.bfloat16)
    grad_prob = jnp.einsum(
        "rhd,rshd->rsh", grad_heads, value_heads, preferred_element_type=jnp.float32
    )
    inner_sum = jnp.sum(probability * grad_prob, axis=1, keepdims=True)
    grad_score = (probability * (grad_prob - inner_sum) * score_scale).astype(jnp.bfloat16)
    grad_query = jnp.einsum(
        "rsh,rshd->rhd", grad_score, key_heads, preferred_element_type=jnp.float32
    )
    grad_query = grad_query.reshape(row_count, model_width).astype(jnp.bfloat16)
    return (grad_query, grad_score, rounded)


def accumulate(per_slot, index_block, operand, table_rows):
    row_count, slot_count, group_count = per_slot.shape
    table_ids = jnp.arange(table_rows, dtype=jnp.int32)[:, None]
    selector = jnp.zeros((group_count, table_rows, row_count), per_slot.dtype)
    for slot_index in range(slot_count):
        matches = table_ids == index_block[:, slot_index][None, :]
        column = jnp.transpose(per_slot[:, slot_index, :])[:, None, :]
        selector = jnp.where(matches[None], column, selector)
    summed = jnp.einsum("gmi,igd->mgd", selector, operand, preferred_element_type=jnp.float32)
    return summed.reshape(table_rows, -1)


def shards(features, cotangent, w_query, w_key, w_value, neighbour, slot_mask, send_rows):
    row_count, model_width = features.shape
    slot_count = neighbour.shape[1]
    halo_rows = send_rows.shape[1]
    head_size = model_width // HEADS
    first_slot = (jnp.arange(slot_count) == 0).astype(jnp.int32)
    usable = jnp.maximum(slot_mask, first_slot[None, :])
    weights = jnp.concatenate([w_query, w_key, w_value], axis=1)
    projected = jnp.dot(features, weights, preferred_element_type=jnp.float32).astype(jnp.bfloat16)
    queries = projected[:, :model_width]
    keyval = projected[:, model_width:]
    outgoing = keyval[send_rows]
    from_lon = extended(outgoing[0:2], (("lon", 0),), 1, True)
    from_lat = extended(outgoing[2:4], (("lat", 0),), 1, False)
    lookup = jnp.concatenate([keyval, from_lon[0], from_lon[3], from_lat[0], from_lat[3]], axis=0)
    table_rows = lookup.shape[0]
    block_rows = min(512, row_count)
    block_count = row_count // block_rows

    def one_block(totals, inputs):
        query_block, grad_block, index_block, mask_block = inputs
        grad_query, grad_score, rounded = attend_back(
            query_block, grad_block, lookup[index_block], mask_block
        )
        per_slot = jnp.concatenate([grad_score, rounded], axis=2)
        operand = jnp.concatenate(
            [
                query_block.reshape(block_rows, HEADS, head_size),
                grad_block.reshape(block_rows, HEADS, head_size),
            ],
            axis=1,
        )
        return (totals + accumulate(per_slot, index_block, operand, table_rows), grad_query)

    totals = jnp.zeros((table_rows, 2 * model_width), jnp.float32)
    totals, grad_query = lax.scan(
        one_block,
        totals,
        (
            queries.reshape(block_count, block_rows, model_width),
            cotangent.reshape(block_count, block_rows, model_width),
            neighbour.reshape(block_count, block_rows, slot_count),
            usable.reshape(block_count, block_rows, slot_count),
        ),
    )
    halo_grad = totals[row_count:].reshape(4, halo_rows, 2 * model_width)
    back_lon = extended(halo_grad[0:2].astype(jnp.bfloat16), (("lon", 0),), 1, True).astype(
        jnp.float32
    )
    back_lat = extended(halo_grad[2:4].astype(jnp.bfloat16), (("lat", 0),), 1, False).astype(
        jnp.float32
    )
    returned = jnp.concatenate([back_lon[0], back_lon[3], back_lat[0], back_lat[3]], axis=0)
    own_grad = totals[:row_count].at[send_rows.reshape(-1)].add(returned)
    stacked = jnp.concatenate(
        [grad_query.reshape(row_count, model_width), own_grad.astype(jnp.bfloat16)], axis=1
    )
    features_grad = lax.dot_general(
        stacked, weights, (((1,), (1,)), ((), ())), preferred_element_type=jnp.float32
    ).astype(jnp.bfloat16)
    partial_terms = lax.dot_general(
        stacked, features, (((0,), (0,)), ((), ())), preferred_element_type=jnp.float32
    )
    summed = lax.psum_scatter(partial_terms, ("lon", "lat"), scatter_dimension=0, tiled=True)
    return (features_grad, summed)


def solution(mesh):
    in_specs = (
        P(("lon", "lat"), None),
        P(("lon", "lat"), None),
        P(),
        P(),
        P(),
        P(("lon", "lat"), None),
        P(("lon", "lat"), None),
        P(("lon", "lat"), None),
    )
    out_specs = (P(("lon", "lat"), None), P(("lon", "lat"), None))
    return jax.shard_map(shards, mesh=mesh, in_specs=in_specs, out_specs=out_specs, check_vma=False)
```

profile of v0, /device:TPU:1, one launch (start us, length us, event | category | flops | bytes accessed | tf_op | source)
XLA Modules:
  0.0 1309.1 jit_solution(13554063573471963596)
XLA Ops:
  34.3 18.3 %gather_fusion.1 = bf16[4096,1024]{1,0:T(8,128)(2,1)} fusion(bf16[768,1024]{1,0:T(8,128)(2,1)S(1)} %copy.42, s32[4096]{0:T(1024)S(1)} %broadcast_clamp_fusion), kind=kCustom, calls=%fused_computation.1 | custom fusion | bytes 16793600 | tf_op jit(solution)/shard_map/while/body/eval_jaxpr/gather | solution.py:91
  131.8 657.5 %fusion = f32[8,512]{1,0:T(8,128)S(1)} fusion(f32[1536,512]{1,0:T(8,128)S(1)} %fusion.69), kind=kCustom, calls=%all-reduce-scatter | all-reduce-scatter fusion | flops 1048577 | bytes 3162112
  789.2 22.4 %collective-permute-start.10 = (f32[8,512]{1,0:T(8,128)S(1)}, f32[8,512]{1,0:T(8,128)S(1)}, u32[]{:S(2)}, u32[]{:S(2)}) collective-permute-start(f32[8,512]{1,0:T(8,128)S(1)} %fusion), channel_id=1, source_target_pairs={{0,3},{1,4},{2,5},{3,6},{4,7},{5,8},{6,9},{7,10},{8,11},{9,12},{10... | collective-permute-start | bytes 49160
  811.6 13.1 %collective-permute-start.11 = (f32[8,512]{1,0:T(8,128)S(1)}, f32[8,512]{1,0:T(8,128)S(1)}, u32[]{:S(2)}, u32[]{:S(2)}) collective-permute-start(f32[8,512]{1,0:T(8,128)S(1)} %fusion), channel_id=1, source_target_pairs={{0,4},{1,5},{2,6},{3,7},{4,8},{5,9},{6,10},{7,11},{8,12},{9,13},{1... | collective-permute-start | bytes 49160
  824.7 13.1 %collective-permute-start.12 = (f32[8,512]{1,0:T(8,128)S(1)}, f32[8,512]{1,0:T(8,128)S(1)}, u32[]{:S(2)}, u32[]{:S(2)}) collective-permute-start(f32[8,512]{1,0:T(8,128)S(1)} %fusion), channel_id=1, source_target_pairs={{0,5},{1,6},{2,7},{3,8},{4,9},{5,10},{6,11},{7,12},{8,13},{9,14},{... | collective-permute-start | bytes 49160
  854.0 13.1 %collective-permute-start.14 = (f32[8,512]{1,0:T(8,128)S(1)}, f32[8,512]{1,0:T(8,128)S(1)}, u32[]{:S(2)}, u32[]{:S(2)}) collective-permute-start(f32[8,512]{1,0:T(8,128)S(1)} %fusion), channel_id=1, source_target_pairs={{0,7},{1,8},{2,9},{3,10},{4,11},{5,12},{6,13},{7,14},{8,15},{9,16}... | collective-permute-start | bytes 49160
  867.2 13.1 %collective-permute-start.15 = (f32[8,512]{1,0:T(8,128)S(1)}, f32[8,512]{1,0:T(8,128)S(1)}, u32[]{:S(2)}, u32[]{:S(2)}) collective-permute-start(f32[8,512]{1,0:T(8,128)S(1)} %fusion), channel_id=1, source_target_pairs={{0,8},{1,9},{2,10},{3,11},{4,12},{5,13},{6,14},{7,15},{8,16},{9,17... | collective-permute-start | bytes 49160
  893.4 13.1 %collective-permute-start.17 = (f32[8,512]{1,0:T(8,128)S(1)}, f32[8,512]{1,0:T(8,128)S(1)}, u32[]{:S(2)}, u32[]{:S(2)}) collective-permute-start(f32[8,512]{1,0:T(8,128)S(1)} %fusion), channel_id=1, source_target_pairs={{0,10},{1,11},{2,12},{3,13},{4,14},{5,15},{6,16},{7,17},{8,18},{9,... | collective-permute-start | bytes 49160
  906.6 13.1 %collective-permute-start.18 = (f32[8,512]{1,0:T(8,128)S(1)}, f32[8,512]{1,0:T(8,128)S(1)}, u32[]{:S(2)}, u32[]{:S(2)}) collective-permute-start(f32[8,512]{1,0:T(8,128)S(1)} %fusion), channel_id=1, source_target_pairs={{0,11},{1,12},{2,13},{3,14},{4,15},{5,16},{6,17},{7,18},{8,19},{9,... | collective-permute-start | bytes 49160
  919.7 13.1 %collective-permute-start.19 = (f32[8,512]{1,0:T(8,128)S(1)}, f32[8,512]{1,0:T(8,128)S(1)}, u32[]{:S(2)}, u32[]{:S(2)}) collective-permute-start(f32[8,512]{1,0:T(8,128)S(1)} %fusion), channel_id=1, source_target_pairs={{0,12},{1,13},{2,14},{3,15},{4,16},{5,17},{6,18},{7,19},{8,20},{9,... | collective-permute-start | bytes 49160
  932.9 13.1 %collective-permute-start.20 = (f32[8,512]{1,0:T(8,128)S(1)}, f32[8,512]{1,0:T(8,128)S(1)}, u32[]{:S(2)}, u32[]{:S(2)}) collective-permute-start(f32[8,512]{1,0:T(8,128)S(1)} %fusion), channel_id=1, source_target_pairs={{0,13},{1,14},{2,15},{3,16},{4,17},{5,18},{6,19},{7,20},{8,21},{9,... | collective-permute-start | bytes 49160
  946.0 13.1 %collective-permute-start.21 = (f32[8,512]{1,0:T(8,128)S(1)}, f32[8,512]{1,0:T(8,128)S(1)}, u32[]{:S(2)}, u32[]{:S(2)}) collective-permute-start(f32[8,512]{1,0:T(8,128)S(1)} %fusion), channel_id=1, source_target_pairs={{0,14},{1,15},{2,16},{3,17},{4,18},{5,19},{6,20},{7,21},{8,22},{9,... | collective-permute-start | bytes 49160
  959.1 13.1 %collective-permute-start.22 = (f32[8,512]{1,0:T(8,128)S(1)}, f32[8,512]{1,0:T(8,128)S(1)}, u32[]{:S(2)}, u32[]{:S(2)}) collective-permute-start(f32[8,512]{1,0:T(8,128)S(1)} %fusion), channel_id=1, source_target_pairs={{0,15},{1,16},{2,17},{3,18},{4,19},{5,20},{6,21},{7,22},{8,23},{9,... | collective-permute-start | bytes 49160
  972.3 13.1 %collective-permute-start.23 = (f32[8,512]{1,0:T(8,128)S(1)}, f32[8,512]{1,0:T(8,128)S(1)}, u32[]{:S(2)}, u32[]{:S(2)}) collective-permute-start(f32[8,512]{1,0:T(8,128)S(1)} %fusion), channel_id=1, source_target_pairs={{0,16},{1,17},{2,18},{3,19},{4,20},{5,21},{6,22},{7,23},{8,24},{9,... | collective-permute-start | bytes 49160
  985.4 13.1 %collective-permute-start.24 = (f32[8,512]{1,0:T(8,128)S(1)}, f32[8,512]{1,0:T(8,128)S(1)}, u32[]{:S(2)}, u32[]{:S(2)}) collective-permute-start(f32[8,512]{1,0:T(8,128)S(1)} %fusion), channel_id=1, source_target_pairs={{0,17},{1,18},{2,19},{3,20},{4,21},{5,22},{6,23},{7,24},{8,25},{9,... | collective-permute-start | bytes 49160
  998.6 13.1 %collective-permute-start.25 = (f32[8,512]{1,0:T(8,128)S(1)}, f32[8,512]{1,0:T(8,128)S(1)}, u32[]{:S(2)}, u32[]{:S(2)}) collective-permute-start(f32[8,512]{1,0:T(8,128)S(1)} %fusion), channel_id=1, source_target_pairs={{0,18},{1,19},{2,20},{3,21},{4,22},{5,23},{6,24},{7,25},{8,26},{9,... | collective-permute-start | bytes 49160
  1011.7 13.1 %collective-permute-start.26 = (f32[8,512]{1,0:T(8,128)S(1)}, f32[8,512]{1,0:T(8,128)S(1)}, u32[]{:S(2)}, u32[]{:S(2)}) collective-permute-start(f32[8,512]{1,0:T(8,128)S(1)} %fusion), channel_id=1, source_target_pairs={{0,19},{1,20},{2,21},{3,22},{4,23},{5,24},{6,25},{7,26},{8,27},{9,... | collective-permute-start | bytes 49160
  1024.8 13.1 %collective-permute-start.27 = (f32[8,512]{1,0:T(8,128)S(1)}, f32[8,512]{1,0:T(8,128)S(1)}, u32[]{:S(2)}, u32[]{:S(2)}) collective-permute-start(f32[8,512]{1,0:T(8,128)S(1)} %fusion), channel_id=1, source_target_pairs={{0,20},{1,21},{2,22},{3,23},{4,24},{5,25},{6,26},{7,27},{8,28},{9,... | collective-permute-start | bytes 49160
  1038.0 13.1 %collective-permute-start.28 = (f32[8,512]{1,0:T(8,128)S(1)}, f32[8,512]{1,0:T(8,128)S(1)}, u32[]{:S(2)}, u32[]{:S(2)}) collective-permute-start(f32[8,512]{1,0:T(8,128)S(1)} %fusion), channel_id=1, source_target_pairs={{0,21},{1,22},{2,23},{3,24},{4,25},{5,26},{6,27},{7,28},{8,29},{9,... | collective-permute-start | bytes 49160
  1051.1 13.1 %collective-permute-start.29 = (f32[8,512]{1,0:T(8,128)S(1)}, f32[8,512]{1,0:T(8,128)S(1)}, u32[]{:S(2)}, u32[]{:S(2)}) collective-permute-start(f32[8,512]{1,0:T(8,128)S(1)} %fusion), channel_id=1, source_target_pairs={{0,22},{1,23},{2,24},{3,25},{4,26},{5,27},{6,28},{7,29},{8,30},{9,... | collective-permute-start | bytes 49160
  1064.3 13.1 %collective-permute-start.30 = (f32[8,512]{1,0:T(8,128)S(1)}, f32[8,512]{1,0:T(8,128)S(1)}, u32[]{:S(2)}, u32[]{:S(2)}) collective-permute-start(f32[8,512]{1,0:T(8,128)S(1)} %fusion), channel_id=1, source_target_pairs={{0,23},{1,24},{2,25},{3,26},{4,27},{5,28},{6,29},{7,30},{8,31},{9,... | collective-permute-start | bytes 49160
  1077.4 13.1 %collective-permute-start.31 = (f32[8,512]{1,0:T(8,128)S(1)}, f32[8,512]{1,0:T(8,128)S(1)}, u32[]{:S(2)}, u32[]{:S(2)}) collective-permute-start(f32[8,512]{1,0:T(8,128)S(1)} %fusion), channel_id=1, source_target_pairs={{0,24},{1,25},{2,26},{3,27},{4,28},{5,29},{6,30},{7,31},{8,32},{9,... | collective-permute-start | bytes 49160
  1090.5 13.1 %collective-permute-start.32 = (f32[8,512]{1,0:T(8,128)S(1)}, f32[8,512]{1,0:T(8,128)S(1)}, u32[]{:S(2)}, u32[]{:S(2)}) collective-permute-start(f32[8,512]{1,0:T(8,128)S(1)} %fusion), channel_id=1, source_target_pairs={{0,25},{1,26},{2,27},{3,28},{4,29},{5,30},{6,31},{7,32},{8,33},{9,... | collective-permute-start | bytes 49160
  1283.4 13.4 %collective-permute-start.9 = (f32[8,512]{1,0:T(8,128)S(1)}, f32[8,512]{1,0:T(8,128)S(1)}, u32[]{:S(2)}, u32[]{:S(2)}) collective-permute-start(f32[8,512]{1,0:T(8,128)S(1)} %fusion), channel_id=1, source_target_pairs={{0,2},{1,3},{2,4},{3,5},{4,6},{5,7},{6,8},{7,9},{8,10},{9,11},{10,... | collective-permute-start | bytes 49160
  (224 shorter events, 332.7 us)
Async XLA Ops:
  789.2 77.9 %collective-permute-start.10 = (f32[8,512]{1,0:T(8,128)S(1)}, f32[8,512]{1,0:T(8,128)S(1)}, u32[]{:S(2)}, u32[]{:S(2)}) collective-permute-start(f32[8,512]{1,0:T(8,128)S(1)} %fusion), channel_id=1, source_target_pairs={{0,3},{1,4},{2,5},{3,6},{4,7},{5,8},{6,9},{7,10},{8,11},{9,12},{10... | collective-permute-start | bytes 49160
  811.6 68.7 %collective-permute-start.11 = (f32[8,512]{1,0:T(8,128)S(1)}, f32[8,512]{1,0:T(8,128)S(1)}, u32[]{:S(2)}, u32[]{:S(2)}) collective-permute-start(f32[8,512]{1,0:T(8,128)S(1)} %fusion), channel_id=1, source_target_pairs={{0,4},{1,5},{2,6},{3,7},{4,8},{5,9},{6,10},{7,11},{8,12},{9,13},{1... | collective-permute-start | bytes 49160
  824.7 68.7 %collective-permute-start.12 = (f32[8,512]{1,0:T(8,128)S(1)}, f32[8,512]{1,0:T(8,128)S(1)}, u32[]{:S(2)}, u32[]{:S(2)}) collective-permute-start(f32[8,512]{1,0:T(8,128)S(1)} %fusion), channel_id=1, source_target_pairs={{0,5},{1,6},{2,7},{3,8},{4,9},{5,10},{6,11},{7,12},{8,13},{9,14},{... | collective-permute-start | bytes 49160
  854.0 65.7 %collective-permute-start.14 = (f32[8,512]{1,0:T(8,128)S(1)}, f32[8,512]{1,0:T(8,128)S(1)}, u32[]{:S(2)}, u32[]{:S(2)}) collective-permute-start(f32[8,512]{1,0:T(8,128)S(1)} %fusion), channel_id=1, source_target_pairs={{0,7},{1,8},{2,9},{3,10},{4,11},{5,12},{6,13},{7,14},{8,15},{9,16}... | collective-permute-start | bytes 49160
  867.2 65.7 %collective-permute-start.15 = (f32[8,512]{1,0:T(8,128)S(1)}, f32[8,512]{1,0:T(8,128)S(1)}, u32[]{:S(2)}, u32[]{:S(2)}) collective-permute-start(f32[8,512]{1,0:T(8,128)S(1)} %fusion), channel_id=1, source_target_pairs={{0,8},{1,9},{2,10},{3,11},{4,12},{5,13},{6,14},{7,15},{8,16},{9,17... | collective-permute-start | bytes 49160
  893.4 65.7 %collective-permute-start.17 = (f32[8,512]{1,0:T(8,128)S(1)}, f32[8,512]{1,0:T(8,128)S(1)}, u32[]{:S(2)}, u32[]{:S(2)}) collective-permute-start(f32[8,512]{1,0:T(8,128)S(1)} %fusion), channel_id=1, source_target_pairs={{0,10},{1,11},{2,12},{3,13},{4,14},{5,15},{6,16},{7,17},{8,18},{9,... | collective-permute-start | bytes 49160
  906.6 65.7 %collective-permute-start.18 = (f32[8,512]{1,0:T(8,128)S(1)}, f32[8,512]{1,0:T(8,128)S(1)}, u32[]{:S(2)}, u32[]{:S(2)}) collective-permute-start(f32[8,512]{1,0:T(8,128)S(1)} %fusion), channel_id=1, source_target_pairs={{0,11},{1,12},{2,13},{3,14},{4,15},{5,16},{6,17},{7,18},{8,19},{9,... | collective-permute-start | bytes 49160
  919.7 65.7 %collective-permute-start.19 = (f32[8,512]{1,0:T(8,128)S(1)}, f32[8,512]{1,0:T(8,128)S(1)}, u32[]{:S(2)}, u32[]{:S(2)}) collective-permute-start(f32[8,512]{1,0:T(8,128)S(1)} %fusion), channel_id=1, source_target_pairs={{0,12},{1,13},{2,14},{3,15},{4,16},{5,17},{6,18},{7,19},{8,20},{9,... | collective-permute-start | bytes 49160
  932.9 65.7 %collective-permute-start.20 = (f32[8,512]{1,0:T(8,128)S(1)}, f32[8,512]{1,0:T(8,128)S(1)}, u32[]{:S(2)}, u32[]{:S(2)}) collective-permute-start(f32[8,512]{1,0:T(8,128)S(1)} %fusion), channel_id=1, source_target_pairs={{0,13},{1,14},{2,15},{3,16},{4,17},{5,18},{6,19},{7,20},{8,21},{9,... | collective-permute-start | bytes 49160
  946.0 65.7 %collective-permute-start.21 = (f32[8,512]{1,0:T(8,128)S(1)}, f32[8,512]{1,0:T(8,128)S(1)}, u32[]{:S(2)}, u32[]{:S(2)}) collective-permute-start(f32[8,512]{1,0:T(8,128)S(1)} %fusion), channel_id=1, source_target_pairs={{0,14},{1,15},{2,16},{3,17},{4,18},{5,19},{6,20},{7,21},{8,22},{9,... | collective-permute-start | bytes 49160
  959.1 65.7 %collective-permute-start.22 = (f32[8,512]{1,0:T(8,128)S(1)}, f32[8,512]{1,0:T(8,128)S(1)}, u32[]{:S(2)}, u32[]{:S(2)}) collective-permute-start(f32[8,512]{1,0:T(8,128)S(1)} %fusion), channel_id=1, source_target_pairs={{0,15},{1,16},{2,17},{3,18},{4,19},{5,20},{6,21},{7,22},{8,23},{9,... | collective-permute-start | bytes 49160
  972.3 65.7 %collective-permute-start.23 = (f32[8,512]{1,0:T(8,128)S(1)}, f32[8,512]{1,0:T(8,128)S(1)}, u32[]{:S(2)}, u32[]{:S(2)}) collective-permute-start(f32[8,512]{1,0:T(8,128)S(1)} %fusion), channel_id=1, source_target_pairs={{0,16},{1,17},{2,18},{3,19},{4,20},{5,21},{6,22},{7,23},{8,24},{9,... | collective-permute-start | bytes 49160
  985.4 65.7 %collective-permute-start.24 = (f32[8,512]{1,0:T(8,128)S(1)}, f32[8,512]{1,0:T(8,128)S(1)}, u32[]{:S(2)}, u32[]{:S(2)}) collective-permute-start(f32[8,512]{1,0:T(8,128)S(1)} %fusion), channel_id=1, source_target_pairs={{0,17},{1,18},{2,19},{3,20},{4,21},{5,22},{6,23},{7,24},{8,25},{9,... | collective-permute-start | bytes 49160
  998.6 65.7 %collective-permute-start.25 = (f32[8,512]{1,0:T(8,128)S(1)}, f32[8,512]{1,0:T(8,128)S(1)}, u32[]{:S(2)}, u32[]{:S(2)}) collective-permute-start(f32[8,512]{1,0:T(8,128)S(1)} %fusion), channel_id=1, source_target_pairs={{0,18},{1,19},{2,20},{3,21},{4,22},{5,23},{6,24},{7,25},{8,26},{9,... | collective-permute-start | bytes 49160
  1011.7 65.7 %collective-permute-start.26 = (f32[8,512]{1,0:T(8,128)S(1)}, f32[8,512]{1,0:T(8,128)S(1)}, u32[]{:S(2)}, u32[]{:S(2)}) collective-permute-start(f32[8,512]{1,0:T(8,128)S(1)} %fusion), channel_id=1, source_target_pairs={{0,19},{1,20},{2,21},{3,22},{4,23},{5,24},{6,25},{7,26},{8,27},{9,... | collective-permute-start | bytes 49160
  1024.8 65.7 %collective-permute-start.27 = (f32[8,512]{1,0:T(8,128)S(1)}, f32[8,512]{1,0:T(8,128)S(1)}, u32[]{:S(2)}, u32[]{:S(2)}) collective-permute-start(f32[8,512]{1,0:T(8,128)S(1)} %fusion), channel_id=1, source_target_pairs={{0,20},{1,21},{2,22},{3,23},{4,24},{5,25},{6,26},{7,27},{8,28},{9,... | collective-permute-start | bytes 49160
  1038.0 65.7 %collective-permute-start.28 = (f32[8,512]{1,0:T(8,128)S(1)}, f32[8,512]{1,0:T(8,128)S(1)}, u32[]{:S(2)}, u32[]{:S(2)}) collective-permute-start(f32[8,512]{1,0:T(8,128)S(1)} %fusion), channel_id=1, source_target_pairs={{0,21},{1,22},{2,23},{3,24},{4,25},{5,26},{6,27},{7,28},{8,29},{9,... | collective-permute-start | bytes 49160
  1051.1 65.7 %collective-permute-start.29 = (f32[8,512]{1,0:T(8,128)S(1)}, f32[8,512]{1,0:T(8,128)S(1)}, u32[]{:S(2)}, u32[]{:S(2)}) collective-permute-start(f32[8,512]{1,0:T(8,128)S(1)} %fusion), channel_id=1, source_target_pairs={{0,22},{1,23},{2,24},{3,25},{4,26},{5,27},{6,28},{7,29},{8,30},{9,... | collective-permute-start | bytes 49160
  1064.3 65.7 %collective-permute-start.30 = (f32[8,512]{1,0:T(8,128)S(1)}, f32[8,512]{1,0:T(8,128)S(1)}, u32[]{:S(2)}, u32[]{:S(2)}) collective-permute-start(f32[8,512]{1,0:T(8,128)S(1)} %fusion), channel_id=1, source_target_pairs={{0,23},{1,24},{2,25},{3,26},{4,27},{5,28},{6,29},{7,30},{8,31},{9,... | collective-permute-start | bytes 49160
  1077.4 65.7 %collective-permute-start.31 = (f32[8,512]{1,0:T(8,128)S(1)}, f32[8,512]{1,0:T(8,128)S(1)}, u32[]{:S(2)}, u32[]{:S(2)}) collective-permute-start(f32[8,512]{1,0:T(8,128)S(1)} %fusion), channel_id=1, source_target_pairs={{0,24},{1,25},{2,26},{3,27},{4,28},{5,29},{6,30},{7,31},{8,32},{9,... | collective-permute-start | bytes 49160
  1090.5 65.7 %collective-permute-start.32 = (f32[8,512]{1,0:T(8,128)S(1)}, f32[8,512]{1,0:T(8,128)S(1)}, u32[]{:S(2)}, u32[]{:S(2)}) collective-permute-start(f32[8,512]{1,0:T(8,128)S(1)} %fusion), channel_id=1, source_target_pairs={{0,25},{1,26},{2,27},{3,28},{4,29},{5,30},{6,31},{7,32},{8,33},{9,... | collective-permute-start | bytes 49160
  1103.7 65.7 %collective-permute-start.33 = (f32[8,512]{1,0:T(8,128)S(1)}, f32[8,512]{1,0:T(8,128)S(1)}, u32[]{:S(2)}, u32[]{:S(2)}) collective-permute-start(f32[8,512]{1,0:T(8,128)S(1)} %fusion), channel_id=1, source_target_pairs={{0,26},{1,27},{2,28},{3,29},{4,30},{5,31},{6,32},{7,33},{8,34},{9,... | collective-permute-start | bytes 49160
  1116.8 65.7 %collective-permute-start.34 = (f32[8,512]{1,0:T(8,128)S(1)}, f32[8,512]{1,0:T(8,128)S(1)}, u32[]{:S(2)}, u32[]{:S(2)}) collective-permute-start(f32[8,512]{1,0:T(8,128)S(1)} %fusion), channel_id=1, source_target_pairs={{0,27},{1,28},{2,29},{3,30},{4,31},{5,32},{6,33},{7,34},{8,35},{9,... | collective-permute-start | bytes 49160
  1130.0 65.7 %collective-permute-start.35 = (f32[8,512]{1,0:T(8,128)S(1)}, f32[8,512]{1,0:T(8,128)S(1)}, u32[]{:S(2)}, u32[]{:S(2)}) collective-permute-start(f32[8,512]{1,0:T(8,128)S(1)} %fusion), channel_id=1, source_target_pairs={{0,28},{1,29},{2,30},{3,31},{4,32},{5,33},{6,34},{7,35},{8,36},{9,... | collective-permute-start | bytes 49160
  (60 other events, 983.3 us)
where the time goes:
time: 1310 us
  blocking collectives  657 us (50%)
  starting transfers between devices  528 us (40%)
  local copies, waits for them, and re-layouts  72.7 us (6%)
  other arithmetic  30.8 us (2%)
  matrix products  15.9 us (1%)
    unnamed x1, blocking collectives  657 us
    unnamed x64, starting transfers between devices  506 us
  transfers between devices with their start and end apart: 72, of which 1 were waited for; matrix products, arithmetic and copies ran while one was open for 2% of the time, Pallas kernels for 0%

commit v1 on v0

v1 whole, which is shorter than its diff:
```python
import jax
import jax.numpy as jnp
import numpy as np
from jax import lax
from jax.experimental import pallas as pl
from jax.experimental.pallas import tpu as pltpu
from jax.sharding import PartitionSpec as P

MESH = pl.DeviceIdType.MESH
F32, BF16, I32 = jnp.float32, jnp.bfloat16, jnp.int32
D, HEADS, SLOTS, ROWS, HALO = 512, 4, 16, 256, 128
HEAD = D // HEADS
TABLE = ROWS + 4 * HALO
SCALE = HEAD ** -0.5
NN = (((1,), (0,)), ((), ()))
NT = (((1,), (1,)), ((), ()))
TN = (((0,), (0,)), ((), ()))
VMEM = pltpu.VMEM
DMA = pltpu.SemaphoreType.DMA


def dot(a, b, dims=NN):
    return lax.dot_general(a, b, dims, preferred_element_type=F32)


def kernel(
    feat, cot, w_query, w_key, w_value, nbr, msk, snd, perm,
    fg_out, dw_out,
    ftab, cot_v, w_v, nbr_v, msk_v, snd_v, perm_v,
    picked, q_v, k_v, v_v, bias, s_v, dp_v, p_v, ds_v, gq_v, gk_v, gv_v, dw_v,
    part, crecv, acc1, precv, acc2, zsend, zrecv, fg_own, fgh_s, fgh_r,
    in_sem, hs_sem, hr_sem, cs_sem, cr_sem, ps_sem, pr_sem, zs_sem, zr_sem, rs_sem, rr_sem,
):
    lon, lat = lax.axis_index("lon"), lax.axis_index("lat")
    z, yh, core = lon // 4, (lon // 2) % 2, lon % 2
    plane = yh * 8 + lat
    partner = (lon + 1 - 2 * core, lat)
    plane_peers = []
    for d in range(1, 16):
        other = (plane + d) % 16
        plane_peers.append((z * 4 + (other // 8) * 2 + core, other % 8))
    z_peers = [(((z + d) % 8) * 4 + yh * 2 + core, lat) for d in range(1, 8)]
    lon_lo, lon_hi = (lon + 31) % 32, (lon + 1) % 32
    lat_lo, lat_hi = (lat + 7) % 8, (lat + 1) % 8
    far = ((lon + 31 + 2 * core) % 32, lat)
    sides = [(lon_lo, lat), (lon_hi, lat), (lon, lat_lo), (lon, lat_hi)]
    lands = (1, 0, 3, 2)

    barrier = pltpu.get_barrier_semaphore()
    peers = [partner, far] + plane_peers + z_peers
    for peer in peers:
        pl.semaphore_signal(barrier, inc=1, device_id=peer, device_id_type=MESH)

    loads = []
    for i, (src, dst) in enumerate(
        [
            (snd, snd_v), (feat, ftab.at[pl.ds(0, ROWS)]), (w_query, w_v.at[0]), (w_key, w_v.at[1]),
            (w_value, w_v.at[2]), (nbr, nbr_v), (msk, msk_v), (cot, cot_v), (perm, perm_v),
        ]
    ):
        load = pltpu.make_async_copy(src, dst, in_sem.at[i])
        load.start()
        loads.append(load)

    loads[0].wait()
    loads[1].wait()
    row_ids = lax.broadcasted_iota(I32, (ROWS, HALO), 0)
    for l in range(4):
        chosen = (row_ids == snd_v[l : l + 1, :]).astype(F32).astype(BF16)
        picked[:, l * HALO : (l + 1) * HALO] = chosen
        fgh_s[l] = dot(chosen, ftab[0:ROWS, :], TN).astype(BF16)
    pl.semaphore_wait(barrier, len(peers))
    halo = []
    for l in range(4):
        copy = pltpu.make_async_remote_copy(
            src_ref=fgh_s.at[l],
            dst_ref=ftab.at[pl.ds(ROWS + lands[l] * HALO, HALO)],
            send_sem=hs_sem.at[l],
            recv_sem=hr_sem.at[lands[l]],
            device_id=sides[l],
            device_id_type=MESH,
        )
        copy.start()
        halo.append(copy)

    loads[2].wait()
    loads[3].wait()
    loads[4].wait()
    own = ftab[0:ROWS, :]
    q_v[...] = dot(own, w_v[0]).astype(BF16)
    k_v[0:ROWS, :] = dot(own, w_v[1]).astype(BF16)
    v_v[0:ROWS, :] = dot(own, w_v[2]).astype(BF16)
    loads[5].wait()
    loads[6].wait()
    slot_ids = lax.broadcasted_iota(I32, (ROWS, SLOTS), 1)
    wanted = jnp.where((msk_v[...] > 0) | (slot_ids == 0), nbr_v[...], -1)
    wanted = jnp.transpose(wanted)
    tile = 32
    for t in range(TABLE // tile):
        ids = lax.broadcasted_iota(I32, (tile, ROWS), 0) + t * tile
        b = jnp.full((tile, ROWS), -1e30, F32)
        for j in range(SLOTS):
            b = jnp.where(ids == wanted[j : j + 1, :], 0.0, b)
        bias[t * tile : (t + 1) * tile, :] = b
    loads[7].wait()
    loads[8].wait()

    def products(lo, hi):
        for h in range(HEADS):
            cols = slice(h * HEAD, (h + 1) * HEAD)
            s_v[h, lo:hi, :] = dot(k_v[lo:hi, cols], q_v[:, cols], NT)
            dp_v[h, lo:hi, :] = dot(v_v[lo:hi, cols], cot_v[:, cols], NT)

    products(0, ROWS)

    for b in range(4):
        halo[b].wait_recv()

    @pl.when(lat == 0)
    def _():
        ftab[ROWS + 2 * HALO : ROWS + 3 * HALO, :] = jnp.zeros((HALO, D), BF16)

    @pl.when(lat == 7)
    def _():
        ftab[ROWS + 3 * HALO : ROWS + 4 * HALO, :] = jnp.zeros((HALO, D), BF16)

    others = ftab[ROWS:TABLE, :]
    k_v[ROWS:TABLE, :] = dot(others, w_v[1]).astype(BF16)
    v_v[ROWS:TABLE, :] = dot(others, w_v[2]).astype(BF16)
    products(ROWS, TABLE)

    step = 64
    for h in range(HEADS):
        top = jnp.full((8, ROWS), -3e38, F32)
        for t in range(0, TABLE, step):
            s = s_v[h, t : t + step, :] + bias[t : t + step, :]
            s_v[h, t : t + step, :] = s
            top = jnp.maximum(top, jnp.max(s.reshape(step // 8, 8, ROWS), axis=0))
        top = jnp.max(top, axis=0, keepdims=True)
        total = jnp.zeros((8, ROWS), F32)
        inner = jnp.zeros((8, ROWS), F32)
        for t in range(0, TABLE, step):
            e = jnp.exp((s_v[h, t : t + step, :] - top) * SCALE)
            s_v[h, t : t + step, :] = e
            total += jnp.sum(e.reshape(step // 8, 8, ROWS), axis=0)
            inner += jnp.sum((e * dp_v[h, t : t + step, :]).reshape(step // 8, 8, ROWS), axis=0)
        inverse = 1.0 / jnp.sum(total, axis=0, keepdims=True)
        inner = jnp.sum(inner, axis=0, keepdims=True) * inverse
        for t in range(0, TABLE, step):
            p = s_v[h, t : t + step, :] * inverse
            p_v[h, t : t + step, :] = p.astype(BF16)
            ds_v[h, t : t + step, :] = (p * (dp_v[h, t : t + step, :] - inner) * SCALE).astype(BF16)
        cols = slice(h * HEAD, (h + 1) * HEAD)
        gv_v[:, cols] = dot(p_v[h], cot_v[:, cols]).astype(BF16)
        gk_v[:, cols] = dot(ds_v[h], q_v[:, cols]).astype(BF16)
        gq_v[:, cols] = dot(ds_v[h], k_v[:, cols], TN).astype(BF16)

    dw_v[0:D, :] = dot(gq_v[...], own, TN).astype(BF16)
    dw_v[D : 2 * D, :] = dot(gk_v[...], ftab[...], TN).astype(BF16)
    dw_v[2 * D : 3 * D, :] = dot(gv_v[...], ftab[...], TN).astype(BF16)

    core_copies = []
    for c in range(2):
        for half in range(2):
            for y in range(2):
                rows = jnp.concatenate(
                    [dw_v[pl.ds((c * 4 + zz) * 192 + y * 96 + half * 48, 48), :] for zz in range(4)], axis=0
                )
                sorted_rows = dot(perm_v[...], rows)
                for k in range(8):
                    block = sorted_rows[k * 24 : (k + 1) * 24, :]
                    block = jnp.concatenate([block[:, 0:256], block[:, 256:512]], axis=0)
                    part[c, half, y * 8 + k] = block.astype(BF16)
        copy = pltpu.make_async_remote_copy(
            src_ref=part.at[c, 1 - core],
            dst_ref=crecv.at[c],
            send_sem=cs_sem.at[c],
            recv_sem=cr_sem.at[c],
            device_id=partner,
            device_id_type=MESH,
        )
        copy.start()
        core_copies.append(copy)

    plane_copies = []
    for c in range(2):
        core_copies[c].wait_recv()
        for k in range(16):
            acc1[c, k] = (part[c, core, k].astype(F32) + crecv[c, k].astype(F32)).astype(BF16)
        for d in range(1, 16):
            copy = pltpu.make_async_remote_copy(
                src_ref=acc1.at[c, (plane + d) % 16],
                dst_ref=precv.at[c, d - 1],
                send_sem=ps_sem.at[c, d - 1],
                recv_sem=pr_sem.at[c, d - 1],
                device_id=plane_peers[d - 1],
                device_id_type=MESH,
            )
            copy.start()
            plane_copies.append(copy)

    for copy in halo:
        copy.wait_send()
    back = []
    for b in range(4):
        rows = slice(ROWS + b * HALO, ROWS + (b + 1) * HALO)
        fgh_s[b] = (dot(gk_v[rows, :], w_v[1], NT) + dot(gv_v[rows, :], w_v[2], NT)).astype(BF16)
        copy = pltpu.make_async_remote_copy(
            src_ref=fgh_s.at[b],
            dst_ref=fgh_r.at[pl.ds(lands[b] * HALO, HALO)],
            send_sem=rs_sem.at[b],
            recv_sem=rr_sem.at[lands[b]],
            device_id=sides[b],
            device_id_type=MESH,
        )
        copy.start()
        back.append(copy)
    fg_own[...] = (
        dot(gq_v[...], w_v[0], NT) + dot(gk_v[0:ROWS, :], w_v[1], NT) + dot(gv_v[0:ROWS, :], w_v[2], NT)
    )

    z_copies = []
    for c in range(2):
        total = acc1[c, plane].astype(F32)
        for d in range(1, 16):
            plane_copies[c * 15 + d - 1].wait_recv()
            total += precv[c, d - 1].astype(F32)
        acc2[0:24, :] = jnp.concatenate([total[0:24, :], total[24:48, :]], axis=1)
        acc2[24:32, :] = jnp.zeros((8, D), F32)
        for zz in range(4):
            zsend[c * 4 + zz] = acc2[zz * 6 : zz * 6 + 8, :]
    for d in range(1, 8):
        copy = pltpu.make_async_remote_copy(
            src_ref=zsend.at[(z + d) % 8],
            dst_ref=zrecv.at[d - 1],
            send_sem=zs_sem.at[d - 1],
            recv_sem=zr_sem.at[d - 1],
            device_id=z_peers[d - 1],
            device_id_type=MESH,
        )
        copy.start()
        z_copies.append(copy)

    for b in range(4):
        back[b].wait_recv()

    @pl.when(lat == 0)
    def _():
        fgh_r[2 * HALO : 3 * HALO, :] = jnp.zeros((HALO, D), BF16)

    @pl.when(lat == 7)
    def _():
        fgh_r[3 * HALO : 4 * HALO, :] = jnp.zeros((HALO, D), BF16)

    fg_out[...] = (fg_own[...] + dot(picked[...], fgh_r[...])).astype(BF16)

    for copy in back + core_copies + plane_copies:
        copy.wait_send()
    total = zsend[z]
    for d in range(1, 8):
        z_copies[d - 1].wait_recv()
        total += zrecv[d - 1]
    dw_out[...] = total[0:6, :]
    for copy in z_copies:
        copy.wait_send()


def sorting():
    source = np.arange(192).reshape(4, 8, 6).transpose(1, 0, 2).reshape(-1)
    return (source[:, None] == np.arange(192)[None, :]).astype(np.float32)


def shards(features, cotangent, w_query, w_key, w_value, neighbour, slot_mask, send_rows):
    whole = pl.BlockSpec(memory_space=VMEM)
    return pl.pallas_call(
        kernel,
        out_shape=(jax.ShapeDtypeStruct((ROWS, D), BF16), jax.ShapeDtypeStruct((6, D), F32)),
        in_specs=[pl.BlockSpec(memory_space=pl.ANY)] * 9,
        out_specs=(whole, whole),
        scratch_shapes=[
            VMEM((TABLE, D), BF16), VMEM((ROWS, D), BF16), VMEM((3, D, D), BF16), VMEM((ROWS, SLOTS), I32),
            VMEM((ROWS, SLOTS), I32), VMEM((4, HALO), I32), VMEM((192, 192), BF16),
            VMEM((ROWS, 4 * HALO), BF16), VMEM((ROWS, D), BF16), VMEM((TABLE, D), BF16), VMEM((TABLE, D), BF16),
            VMEM((TABLE, ROWS), F32), VMEM((HEADS, TABLE, ROWS), F32), VMEM((HEADS, TABLE, ROWS), F32),
            VMEM((HEADS, TABLE, ROWS), BF16), VMEM((HEADS, TABLE, ROWS), BF16),
            VMEM((ROWS, D), BF16), VMEM((TABLE, D), BF16), VMEM((TABLE, D), BF16), VMEM((3 * D, D), BF16),
            VMEM((2, 2, 16, 48, 256), BF16), VMEM((2, 16, 48, 256), BF16), VMEM((2, 16, 48, 256), BF16),
            VMEM((2, 15, 48, 256), BF16), VMEM((32, D), F32), VMEM((8, 8, D), F32), VMEM((7, 8, D), F32),
            VMEM((ROWS, D), F32), VMEM((4, HALO, D), BF16), VMEM((4 * HALO, D), BF16),
            DMA((9,)), DMA((4,)), DMA((4,)), DMA((2,)), DMA((2,)), DMA((2, 15)), DMA((2, 15)),
            DMA((7,)), DMA((7,)), DMA((4,)), DMA((4,)),
        ],
        compiler_params=pltpu.CompilerParams(
            collective_id=0, has_side_effects=True, vmem_limit_bytes=48 * 1024 * 1024
        ),
        name="mesh_attention_backward",
    )(
        features, cotangent, w_query, w_key, w_value, neighbour, slot_mask, send_rows,
        jnp.asarray(sorting(), BF16),
    )


def solution(mesh):
    rows = P(("lon", "lat"), None)
    return jax.shard_map(
        shards,
        mesh=mesh,
        in_specs=(rows, rows, P(), P(), P(), rows, rows, rows),
        out_specs=(rows, rows),
        check_vma=False,
    )
```

time: 1310 us -> 52.9 us (0.04)
  blocking collectives: 657 us -> 0 us
  starting transfers between devices: 528 us -> 0 us
  local copies, waits for them, and re-layouts: 72.7 us -> 7.83 us
  Pallas kernels: 0 us -> 44 us
  other arithmetic: 30.8 us -> 0 us
  matrix products: 15.9 us -> 0 us
    unnamed x1 -> x0, blocking collectives: 657 us -> none
    unnamed x64 -> x0, starting transfers between devices: 506 us -> none
    pallas_call x0 -> x1, Pallas kernels: none -> 44 us  [shards(): pl.pallas_call(kernel, out_shape=(jax.ShapeDtypeStruct((ROWS, D), BF16),...]
    ppermute x8 -> x0, starting transfers between devices: 21.1 us -> none  [the longest x4 15.9 us: extended(): lax.ppermute(tail, axis, [(i, (i + 1) % count) for i in range(ends)])]
    gather x2 -> x0, local copies, waits for them, and re-layouts: 20.4 us -> none  [the longest x1 18.3 us: one_block(): lookup[index_block]]
    unnamed x41 -> x20, local copies, waits for them, and re-layouts: 25.4 us -> 7.83 us
    dot_general x5 -> x0, matrix products: 15.9 us -> none  [the longest x1 7.31 us: accumulate(): jnp.einsum('gmi,igd->mgd', selector, operand, preferred_element_type=jnp....]
    reshape x2 -> x0, local copies, waits for them, and re-layouts: 13.9 us -> none  [the longest x1 7.04 us: attend_back(): gathered[:, :, model_width:]]
  transfers between devices with their start and end apart: 72 -> 0, of which waited for: 1 -> 0; matrix products, arithmetic and copies ran while one was open for 2% -> 0% of each run, Pallas kernels for 0% -> 0%
where the time goes in v1:
time: 52.9 us; the launch traced here: 52.5 us
  Pallas kernels  44 us (83%)
  local copies, waits for them, and re-layouts  7.83 us (15%)
  between operations  0.68 us (1%)
    pallas_call x1, Pallas kernels, shards(): pl.pallas_call(kernel, out_shape=(jax.ShapeDtypeStruct((ROWS, D), BF16),...  44 us
    unnamed x20, local copies, waits for them, and re-layouts  7.83 us

profile of v1, /device:TPU:1, one launch (start us, length us, event | category | flops | bytes accessed | tf_op | source)
XLA Modules:
  0.0 52.5 jit_solution(10033073988447382692)
XLA Ops:
  0.6 0.0 copy-start.7
  0.6 0.0 copy-start.3
  0.6 0.9 %copy.11.nbr = s32[256,16]{1,0:T(8,128)S(1)} copy(s32[256,16]{0,1:T(8,128)} %param.14) | data formatting | bytes 32768 | tf_op args[5]
  1.5 0.0 copy-done.7
  1.5 0.0 copy-start.6
  1.5 0.1 copy.12.msk
  1.6 0.0 copy-done.3
  1.6 0.6 %copy-done.6 = s32[4,128]{1,0:T(4,128)S(1)} copy-done((s32[4,128]{1,0:T(4,128)S(1)}, s32[4,128]{1,0:T(4,128)}, u32[]{:S(2)}) %copy-start.6) | copy-done | bytes 2072
  2.2 0.0 copy-start
  2.2 1.0 %copy-done = bf16[512,512]{1,0:T(8,128)(2,1)S(1)} copy-done((bf16[512,512]{1,0:T(8,128)(2,1)S(1)}, bf16[512,512]{1,0:T(8,128)(2,1)}, u32[]{:S(2)}) %copy-start) | copy-done | bytes 524312
  3.3 0.0 copy-start.1
  3.3 1.0 %copy-done.1 = bf16[512,512]{1,0:T(8,128)(2,1)S(1)} copy-done((bf16[512,512]{1,0:T(8,128)(2,1)S(1)}, bf16[512,512]{1,0:T(8,128)(2,1)}, u32[]{:S(2)}) %copy-start.1) | copy-done | bytes 524312
  4.3 0.0 copy-start.2
  4.3 1.0 %copy-done.2 = bf16[512,512]{1,0:T(8,128)(2,1)S(1)} copy-done((bf16[512,512]{1,0:T(8,128)(2,1)S(1)}, bf16[512,512]{1,0:T(8,128)(2,1)}, u32[]{:S(2)}) %copy-start.2) | copy-done | bytes 524312
  5.3 0.0 copy-start.4
  5.3 0.9 %copy-done.4 = bf16[256,512]{1,0:T(8,128)(2,1)S(1)} copy-done((bf16[256,512]{1,0:T(8,128)(2,1)S(1)}, bf16[256,512]{1,0:T(8,128)(2,1)}, u32[]{:S(2)}) %copy-start.4) | copy-done | bytes 262168
  6.3 0.0 copy-start.5
  6.3 0.9 %copy-done.5 = bf16[192,192]{1,0:T(8,128)(2,1)S(1)} copy-done((bf16[192,192]{1,0:T(8,128)(2,1)S(1)}, bf16[192,192]{1,0:T(8,128)(2,1)}, u32[]{:S(2)}) %copy-start.5) | copy-done | bytes 73752
  7.2 44.0 %mesh_attention_backward.1 = (bf16[256,512]{1,0:T(8,128)(2,1)S(1)}, f32[6,512]{1,0:T(8,128)S(1)}) custom-call(bf16[256,512]{1,0:T(8,128)(2,1)S(1)} %copy-done.3, bf16[256,512]{1,0:T(8,128)(2,1)S(1)} %copy-done.4, bf16[512,512]{1,0:T(8,128)(2,1)S(1)} %copy-done, bf16[512,512]{1,0:T(8,128)(2,1)S(1)} %copy-done.1, bf16[512,512]{1,0:T(8,128)(2,1)S(1)} %copy-done.2, ...), custom_call_target="tpu_custom_call" | custom-call | tf_op jit(solution)/shard_map/mesh_attention_backward/pallas_call | solution.py:275
  51.2 0.7 %copy.15 = bf16[256,512]{1,0:T(8,128)(2,1)} copy(bf16[256,512]{1,0:T(8,128)(2,1)S(1)} %get-tuple-element.4) | data formatting | bytes 524288
  51.9 0.6 %copy.16 = f32[6,512]{1,0:T(8,128)} copy(f32[6,512]{1,0:T(8,128)S(1)} %get-tuple-element.5) | data formatting | bytes 24576
Async XLA Ops:
  0.6 0.9 %copy-start.7 = (s32[256,16]{0,1:T(8,128)S(1)}, s32[256,16]{0,1:T(8,128)}, u32[]{:S(2)}) copy-start(s32[256,16]{0,1:T(8,128)} %param.15) | copy-start | bytes 49156
  0.6 1.0 %copy-start.3 = (bf16[256,512]{1,0:T(8,128)(2,1)S(1)}, bf16[256,512]{1,0:T(8,128)(2,1)}, u32[]{:S(2)}) copy-start(bf16[256,512]{1,0:T(8,128)(2,1)} %feat.1) | copy-start | bytes 786436
  1.5 0.7 %copy-start.6 = (s32[4,128]{1,0:T(4,128)S(1)}, s32[4,128]{1,0:T(4,128)}, u32[]{:S(2)}) copy-start(s32[4,128]{1,0:T(4,128)} %snd.1) | copy-start | bytes 6148
  2.2 1.0 %copy-start = (bf16[512,512]{1,0:T(8,128)(2,1)S(1)}, bf16[512,512]{1,0:T(8,128)(2,1)}, u32[]{:S(2)}) copy-start(bf16[512,512]{1,0:T(8,128)(2,1)} %w_query.1) | copy-start | bytes 1572868
  3.3 1.0 %copy-start.1 = (bf16[512,512]{1,0:T(8,128)(2,1)S(1)}, bf16[512,512]{1,0:T(8,128)(2,1)}, u32[]{:S(2)}) copy-start(bf16[512,512]{1,0:T(8,128)(2,1)} %w_key.1) | copy-start | bytes 1572868
  4.3 1.0 %copy-start.2 = (bf16[512,512]{1,0:T(8,128)(2,1)S(1)}, bf16[512,512]{1,0:T(8,128)(2,1)}, u32[]{:S(2)}) copy-start(bf16[512,512]{1,0:T(8,128)(2,1)} %w_value.1) | copy-start | bytes 1572868
  5.3 0.9 %copy-start.4 = (bf16[256,512]{1,0:T(8,128)(2,1)S(1)}, bf16[256,512]{1,0:T(8,128)(2,1)}, u32[]{:S(2)}) copy-start(bf16[256,512]{1,0:T(8,128)(2,1)} %cot.1) | copy-start | bytes 786436
  6.3 0.9 %copy-start.5 = (bf16[192,192]{1,0:T(8,128)(2,1)S(1)}, bf16[192,192]{1,0:T(8,128)(2,1)}, u32[]{:S(2)}) copy-start(bf16[192,192]{1,0:T(8,128)(2,1)} %constant.2.clone.perm) | copy-start | bytes 221188

commit v2 on v1

v2 whole, which is shorter than its diff:
```python
import jax
import jax.numpy as jnp
import numpy as np
from jax import lax
from jax.experimental import pallas as pl
from jax.experimental.pallas import tpu as pltpu
from jax.sharding import PartitionSpec as P

MESH = pl.DeviceIdType.MESH
F32, BF16, I32 = jnp.float32, jnp.bfloat16, jnp.int32
D, HEADS, SLOTS, ROWS, HALO = 512, 4, 16, 256, 128
HEAD = D // HEADS
TABLE = ROWS + 4 * HALO
SCALE = HEAD ** -0.5
NN = (((1,), (0,)), ((), ()))
NT = (((1,), (1,)), ((), ()))
TN = (((0,), (0,)), ((), ()))
VMEM = pltpu.VMEM
OFFSETS = sorted(
    ((dy, dx) for dy in range(4) for dx in range(4) if dy or dx),
    key=lambda at: -(min(at[0], 4 - at[0]) + min(at[1], 4 - at[1])),
)
DMA = pltpu.SemaphoreType.DMA


def dot(a, b, dims=NN):
    return lax.dot_general(a, b, dims, preferred_element_type=F32)


def kernel(
    feat, cot, w_query, w_key, w_value, nbr, msk, snd, perm,
    fg_out, dw_out,
    ftab, cot_v, w_v, nbr_v, msk_v, snd_v, perm_v,
    picked, q_v, k_v, v_v, bias, s_v, dp_v, p_v, ds_v, gq_v, gk_v, gv_v, dw_v,
    part, crecv, acc1, precv, acc2, zsend, zrecv, fg_own, fgh_s, fgh_r,
    in_sem, hs_sem, hr_sem, cs_sem, cr_sem, ps_sem, pr_sem, zs_sem, zr_sem, rs_sem, rr_sem,
):
    lon, lat = lax.axis_index("lon"), lax.axis_index("lat")
    z, core = lon // 4, lon % 2
    y, x = ((lon // 2) % 2) * 2 + lat // 4, lat % 4
    plane = y * 4 + x
    partner = (lon + 1 - 2 * core, lat)
    planes, plane_peers = [], []
    for dy, dx in OFFSETS:
        other_y, other_x = (y + dy) % 4, (x + dx) % 4
        planes.append(other_y * 4 + other_x)
        plane_peers.append((z * 4 + (other_y // 2) * 2 + core, (other_y % 2) * 4 + other_x))
    z_peers = [(other * 4 + lon % 4, lat) for other in range(8)]
    lat_lo, lat_hi = (lat + 7) % 8, (lat + 1) % 8
    far = ((lon + 31 + 2 * core) % 32, lat)
    sides = [(core, 1 - core, far), (2, 3, (lon, lat_lo)), (3, 2, (lon, lat_hi)), (1 - core, core, partner)]

    def load(i, src, dst):
        copy = pltpu.make_async_copy(src, dst, in_sem.at[i])
        copy.start()
        return copy

    rows_in = [load(0, snd, snd_v), load(1, feat, ftab.at[pl.ds(0, ROWS)])]
    barrier = pltpu.get_barrier_semaphore()
    peers = [far, partner] + plane_peers + [(((z + d) % 8) * 4 + lon % 4, lat) for d in (4, 3, 5, 2, 6, 1, 7)]
    for peer in peers:
        pl.semaphore_signal(barrier, inc=1, device_id=peer, device_id_type=MESH)

    for copy in rows_in:
        copy.wait()
    weights_in = [load(2, w_query, w_v.at[0]), load(3, w_key, w_v.at[1]), load(4, w_value, w_v.at[2])]
    slots_in = [load(5, nbr, nbr_v), load(6, msk, msk_v)]
    rest_in = [load(7, cot, cot_v), load(8, perm, perm_v)]
    row_ids = lax.broadcasted_iota(I32, (ROWS, HALO), 0)
    for l in range(4):
        chosen = (row_ids == snd_v[l : l + 1, :]).astype(F32).astype(BF16)
        picked[:, l * HALO : (l + 1) * HALO] = chosen
        fgh_s[l] = dot(chosen, ftab[0:ROWS, :], TN).astype(BF16)
    pl.semaphore_wait(barrier, len(peers))
    halo = []
    for i, (l, block, device) in enumerate(sides):
        copy = pltpu.make_async_remote_copy(
            src_ref=fgh_s.at[l],
            dst_ref=ftab.at[pl.ds(ROWS + block * HALO, HALO)],
            send_sem=hs_sem.at[i],
            recv_sem=hr_sem.at[i],
            device_id=device,
            device_id_type=MESH,
        )
        copy.start()
        halo.append(copy)

    for copy in weights_in:
        copy.wait()
    own = ftab[0:ROWS, :]
    q_v[...] = dot(own, w_v[0]).astype(BF16)
    k_v[0:ROWS, :] = dot(own, w_v[1]).astype(BF16)
    v_v[0:ROWS, :] = dot(own, w_v[2]).astype(BF16)
    for copy in slots_in:
        copy.wait()
    slot_ids = lax.broadcasted_iota(I32, (SLOTS, ROWS), 0)
    wanted = jnp.where((msk_v[...] > 0) | (slot_ids == 0), nbr_v[...], -1)
    tile = 32
    for t in range(TABLE // tile):
        ids = lax.broadcasted_iota(I32, (tile, ROWS), 0) + t * tile
        b = jnp.full((tile, ROWS), -1e30, F32)
        for j in range(SLOTS):
            b = jnp.where(ids == wanted[j : j + 1, :], 0.0, b)
        bias[t * tile : (t + 1) * tile, :] = b
    for copy in rest_in:
        copy.wait()

    step = 64
    tops = [jnp.full((8, ROWS), -3e38, F32) for _ in range(HEADS)]

    def products(lo, hi):
        for h in range(HEADS):
            cols = slice(h * HEAD, (h + 1) * HEAD)
            s_v[h, lo:hi, :] = dot(k_v[lo:hi, cols], q_v[:, cols], NT)
            dp_v[h, lo:hi, :] = dot(v_v[lo:hi, cols], cot_v[:, cols], NT)
            for t in range(lo, hi, step):
                s = s_v[h, t : t + step, :] + bias[t : t + step, :]
                s_v[h, t : t + step, :] = s
                tops[h] = jnp.maximum(tops[h], jnp.max(s.reshape(step // 8, 8, ROWS), axis=0))

    products(0, ROWS)

    for copy in halo:
        copy.wait_recv()

    @pl.when(lat == 0)
    def _():
        ftab[ROWS + 2 * HALO : ROWS + 3 * HALO, :] = jnp.zeros((HALO, D), BF16)

    @pl.when(lat == 7)
    def _():
        ftab[ROWS + 3 * HALO : ROWS + 4 * HALO, :] = jnp.zeros((HALO, D), BF16)

    others = ftab[ROWS:TABLE, :]
    k_v[ROWS:TABLE, :] = dot(others, w_v[1]).astype(BF16)
    v_v[ROWS:TABLE, :] = dot(others, w_v[2]).astype(BF16)
    products(ROWS, TABLE)

    for h in range(HEADS):
        cols = slice(h * HEAD, (h + 1) * HEAD)
        top = jnp.max(tops[h], axis=0, keepdims=True)
        total = jnp.zeros((8, ROWS), F32)
        inner = jnp.zeros((8, ROWS), F32)
        for t in range(0, TABLE, step):
            e = jnp.exp((s_v[h, t : t + step, :] - top) * SCALE)
            s_v[h, t : t + step, :] = e
            total += jnp.sum(e.reshape(step // 8, 8, ROWS), axis=0)
            inner += jnp.sum((e * dp_v[h, t : t + step, :]).reshape(step // 8, 8, ROWS), axis=0)
        inverse = 1.0 / jnp.sum(total, axis=0, keepdims=True)
        inner = jnp.sum(inner, axis=0, keepdims=True) * inverse
        for t in range(0, TABLE, step):
            p = s_v[h, t : t + step, :] * inverse
            p_v[h, t : t + step, :] = p.astype(BF16)
            ds_v[h, t : t + step, :] = (p * (dp_v[h, t : t + step, :] - inner) * SCALE).astype(BF16)
        gq_v[:, cols] = dot(ds_v[h], k_v[:, cols], TN).astype(BF16)
        if h < 2:
            gk_v[:, cols] = dot(ds_v[h], q_v[:, cols]).astype(BF16)

    def to_partner(c):
        for half in range(2):
            for y_hi in range(2):
                rows = jnp.concatenate(
                    [dw_v[pl.ds((c * 4 + zz) * 192 + y_hi * 96 + half * 48, 48), :] for zz in range(4)], axis=0
                )
                sorted_rows = dot(perm_v[...], rows)
                for k in range(8):
                    block = sorted_rows[k * 24 : (k + 1) * 24, :]
                    block = jnp.concatenate([block[:, 0:256], block[:, 256:512]], axis=0)
                    part[c, half, y_hi * 8 + k] = block.astype(BF16)
        copy = pltpu.make_async_remote_copy(
            src_ref=part.at[c, 1 - core],
            dst_ref=crecv.at[c],
            send_sem=cs_sem.at[c],
            recv_sem=cr_sem.at[c],
            device_id=partner,
            device_id_type=MESH,
        )
        copy.start()
        return copy

    def to_plane(c, from_partner):
        from_partner.wait_recv()
        copies = []
        for i, other in enumerate(planes):
            acc1[c, other] = (part[c, core, other].astype(F32) + crecv[c, other].astype(F32)).astype(BF16)
            copy = pltpu.make_async_remote_copy(
                src_ref=acc1.at[c, other],
                dst_ref=precv.at[c, i],
                send_sem=ps_sem.at[c, i],
                recv_sem=pr_sem.at[c, i],
                device_id=plane_peers[i],
                device_id_type=MESH,
            )
            copy.start()
            copies.append(copy)
        return copies

    def to_z(c, from_plane):
        total = part[c, core, plane].astype(F32) + crecv[c, plane].astype(F32)
        for i, copy in enumerate(from_plane):
            copy.wait_recv()
            total += precv[c, i].astype(F32)
        acc2[c, 0:24, :] = jnp.concatenate([total[0:24, :], total[24:48, :]], axis=1)
        acc2[c, 24:32, :] = jnp.zeros((8, D), F32)
        copies = []
        for zz in range(4):
            other = c * 4 + zz
            rows = acc2[c, zz * 6 : zz * 6 + 8, :]
            zsend[other] = jnp.concatenate([rows[:, 0:256], rows[:, 256:512]], axis=0).astype(BF16)
            copy = pltpu.make_async_remote_copy(
                src_ref=zsend.at[other],
                dst_ref=zrecv.at[z],
                send_sem=zs_sem.at[other],
                recv_sem=zr_sem.at[z],
                device_id=z_peers[other],
                device_id_type=MESH,
            )
            pl.when(z != other)(copy.start)
        return copies

    dw_v[0:D, :] = dot(gq_v[...], own, TN).astype(BF16)
    dw_v[D : D + 256, :] = dot(gk_v[:, 0:256], ftab[...], TN).astype(BF16)
    core_a = to_partner(0)
    for h in range(HEADS):
        cols = slice(h * HEAD, (h + 1) * HEAD)
        gv_v[:, cols] = dot(p_v[h], cot_v[:, cols]).astype(BF16)
        if h >= 2:
            gk_v[:, cols] = dot(ds_v[h], q_v[:, cols]).astype(BF16)
    dw_v[D + 256 : 2 * D, :] = dot(gk_v[:, 256:512], ftab[...], TN).astype(BF16)
    dw_v[2 * D : 3 * D, :] = dot(gv_v[...], ftab[...], TN).astype(BF16)
    plane_a = to_plane(0, core_a)
    core_b = to_partner(1)
    fg_own[...] = (
        dot(gq_v[...], w_v[0], NT) + dot(gk_v[0:ROWS, :], w_v[1], NT) + dot(gv_v[0:ROWS, :], w_v[2], NT)
    )
    plane_b = to_plane(1, core_b)

    for copy in halo:
        copy.wait_send()
    for b in range(4):
        rows = slice(ROWS + b * HALO, ROWS + (b + 1) * HALO)
        fgh_s[b] = (dot(gk_v[rows, :], w_v[1], NT) + dot(gv_v[rows, :], w_v[2], NT)).astype(BF16)
    to_z(0, plane_a)
    back = []
    for i, (b, block, device) in enumerate(sides):
        copy = pltpu.make_async_remote_copy(
            src_ref=fgh_s.at[b],
            dst_ref=fgh_r.at[pl.ds(block * HALO, HALO)],
            send_sem=rs_sem.at[i],
            recv_sem=rr_sem.at[i],
            device_id=device,
            device_id_type=MESH,
        )
        copy.start()
        back.append(copy)
    to_z(1, plane_b)

    for copy in back:
        copy.wait_recv()

    @pl.when(lat == 0)
    def _():
        fgh_r[2 * HALO : 3 * HALO, :] = jnp.zeros((HALO, D), BF16)

    @pl.when(lat == 7)
    def _():
        fgh_r[3 * HALO : 4 * HALO, :] = jnp.zeros((HALO, D), BF16)

    fg_out[...] = (fg_own[...] + dot(picked[...], fgh_r[...])).astype(BF16)

    for copy in back + [core_a, core_b] + plane_a + plane_b:
        copy.wait_send()
    zrecv[z] = zsend[z]
    for other in range(8):
        copy = pltpu.make_async_remote_copy(
            src_ref=zsend.at[other],
            dst_ref=zrecv.at[other],
            send_sem=zs_sem.at[other],
            recv_sem=zr_sem.at[other],
            device_id=z_peers[other],
            device_id_type=MESH,
        )
        pl.when(z != other)(copy.wait)
    total = zrecv[0].astype(F32)
    for other in range(1, 8):
        total += zrecv[other].astype(F32)
    dw_out[...] = jnp.concatenate([total[0:6, :], total[8:14, :]], axis=1)


def sorting():
    source = np.arange(192).reshape(4, 8, 6).transpose(1, 0, 2).reshape(-1)
    return (source[:, None] == np.arange(192)[None, :]).astype(np.float32)


def shards(features, cotangent, w_query, w_key, w_value, neighbour, slot_mask, send_rows):
    whole = pl.BlockSpec(memory_space=VMEM)
    return pl.pallas_call(
        kernel,
        out_shape=(jax.ShapeDtypeStruct((ROWS, D), BF16), jax.ShapeDtypeStruct((6, D), F32)),
        in_specs=[pl.BlockSpec(memory_space=pl.ANY)] * 9,
        out_specs=(whole, whole),
        scratch_shapes=[
            VMEM((TABLE, D), BF16), VMEM((ROWS, D), BF16), VMEM((3, D, D), BF16), VMEM((SLOTS, ROWS), I32),
            VMEM((SLOTS, ROWS), I32), VMEM((4, HALO), I32), VMEM((192, 192), BF16),
            VMEM((ROWS, 4 * HALO), BF16), VMEM((ROWS, D), BF16), VMEM((TABLE, D), BF16), VMEM((TABLE, D), BF16),
            VMEM((TABLE, ROWS), F32), VMEM((HEADS, TABLE, ROWS), F32), VMEM((HEADS, TABLE, ROWS), F32),
            VMEM((HEADS, TABLE, ROWS), BF16), VMEM((HEADS, TABLE, ROWS), BF16),
            VMEM((ROWS, D), BF16), VMEM((TABLE, D), BF16), VMEM((TABLE, D), BF16), VMEM((3 * D, D), BF16),
            VMEM((2, 2, 16, 48, 256), BF16), VMEM((2, 16, 48, 256), BF16), VMEM((2, 16, 48, 256), BF16),
            VMEM((2, 15, 48, 256), BF16), VMEM((2, 32, D), F32), VMEM((8, 16, 256), BF16), VMEM((8, 16, 256), BF16),
            VMEM((ROWS, D), F32), VMEM((4, HALO, D), BF16), VMEM((4 * HALO, D), BF16),
            DMA((9,)), DMA((4,)), DMA((4,)), DMA((2,)), DMA((2,)), DMA((2, 15)), DMA((2, 15)),
            DMA((8,)), DMA((8,)), DMA((4,)), DMA((4,)),
        ],
        compiler_params=pltpu.CompilerParams(
            collective_id=0, has_side_effects=True, vmem_limit_bytes=60 * 1024 * 1024
        ),
        name="mesh_attention_backward",
    )(
        features, cotangent, w_query, w_key, w_value, neighbour.T, slot_mask.T, send_rows,
        jnp.asarray(sorting(), BF16),
    )


def solution(mesh):
    rows = P(("lon", "lat"), None)
    return jax.shard_map(
        shards,
        mesh=mesh,
        in_specs=(rows, rows, P(), P(), P(), rows, rows, rows),
        out_specs=(rows, rows),
        check_vma=False,
    )
```

time: 52.9 us -> 45.1 us (0.85)
  local copies, waits for them, and re-layouts: 7.83 us -> 2.28 us
  Pallas kernels: 44 us -> 42.1 us
    unnamed x20 -> x4, local copies, waits for them, and re-layouts: 7.83 us -> 2.28 us
    pallas_call x1, Pallas kernels: 44 us -> 42.1 us  [shards(): pl.pallas_call(kernel, out_shape=(jax.ShapeDtypeStruct((ROWS, D), BF16),...]
where the time goes in v2:
time: 45.1 us; the launch traced here: 45 us
  Pallas kernels  42.1 us (93%)
  local copies, waits for them, and re-layouts  2.28 us (5%)
  between operations  0.65 us (1%)
    pallas_call x1, Pallas kernels, shards(): pl.pallas_call(kernel, out_shape=(jax.ShapeDtypeStruct((ROWS, D), BF16),...  42.1 us
    unnamed x4, local copies, waits for them, and re-layouts  2.28 us

profile of v2, /device:TPU:1, one launch (start us, length us, event | category | flops | bytes accessed | tf_op | source)
XLA Modules:
  0.0 45.0 jit_solution(437628236074450038)
XLA Ops:
  0.6 42.1 %mesh_attention_backward.1 = (bf16[256,512]{1,0:T(8,128)(2,1)}, f32[6,512]{1,0:T(8,128)}) custom-call(bf16[256,512]{1,0:T(8,128)(2,1)} %feat.1, bf16[256,512]{1,0:T(8,128)(2,1)} %cot.1, bf16[512,512]{1,0:T(8,128)(2,1)} %w_query.1, bf16[512,512]{1,0:T(8,128)(2,1)} %w_key.1, bf16[512,512]{1,0:T(8,128)(2,1)} %w_value.1, s32[16,256]{1,0:T(8,128)} %bitcast.2, ...), custom_call_target="tpu_custom_call" | custom-call | tf_op jit(solution)/shard_map/mesh_attention_backward/pallas_call | solution.py:297
  42.7 0.0 copy-start
  42.7 1.7 %copy.13 = bf16[256,512]{1,0:T(8,128)(2,1)} copy(bf16[256,512]{1,0:T(8,128)(2,1)} %get-tuple-element.4) | data formatting | bytes 524288
  44.4 0.0 copy-done
  44.4 0.6 %copy.14 = f32[6,512]{1,0:T(8,128)} copy(f32[6,512]{1,0:T(8,128)S(1)} %copy-done) | data formatting | bytes 24576
Async XLA Ops:
  42.7 1.7 %copy-start = (f32[6,512]{1,0:T(8,128)S(1)}, f32[6,512]{1,0:T(8,128)}, u32[]{:S(2)}) copy-start(f32[6,512]{1,0:T(8,128)} %get-tuple-element.5) | copy-start | bytes 36868

commit v3 on v2

--- a/solution.py
+++ b/solution.py
@@ -48,7 +48,16 @@
     z_peers = [(other * 4 + lon % 4, lat) for other in range(8)]
     lat_lo, lat_hi = (lat + 7) % 8, (lat + 1) % 8
     far = ((lon + 31 + 2 * core) % 32, lat)
-    sides = [(core, 1 - core, far), (2, 3, (lon, lat_lo)), (3, 2, (lon, lat_hi)), (1 - core, core, partner)]
+    sides = [partner, (lon, lat_lo), (lon, lat_hi), far]
+    lands = (0, 2, 1, 3)
+
+    def on_side(b, act):
+        if b == 1:
+            pl.when(lat > 0)(act)
+        elif b == 2:
+            pl.when(lat < 7)(act)
+        else:
+            act()
 
     def load(i, src, dst):
         copy = pltpu.make_async_copy(src, dst, in_sem.at[i])
@@ -67,23 +76,27 @@
     slots_in = [load(5, nbr, nbr_v), load(6, msk, msk_v)]
     rest_in = [load(7, cot, cot_v), load(8, perm, perm_v)]
     row_ids = lax.broadcasted_iota(I32, (ROWS, HALO), 0)
-    for l in range(4):
-        chosen = (row_ids == snd_v[l : l + 1, :]).astype(F32).astype(BF16)
-        picked[:, l * HALO : (l + 1) * HALO] = chosen
-        fgh_s[l] = dot(chosen, ftab[0:ROWS, :], TN).astype(BF16)
+    below, above = snd_v[0:1, :], snd_v[1:2, :]
+    lists = [jnp.where(core == 0, above, below), snd_v[2:3, :], snd_v[3:4, :], jnp.where(core == 0, below, above)]
+    for b in (3, 1, 2, 0):
+        chosen = (row_ids == lists[b]).astype(F32).astype(BF16)
+        picked[:, b * HALO : (b + 1) * HALO] = chosen
+        fgh_s[b] = dot(chosen, ftab[0:ROWS, :], TN).astype(BF16)
     pl.semaphore_wait(barrier, len(peers))
     halo = []
-    for i, (l, block, device) in enumerate(sides):
-        copy = pltpu.make_async_remote_copy(
-            src_ref=fgh_s.at[l],
-            dst_ref=ftab.at[pl.ds(ROWS + block * HALO, HALO)],
-            send_sem=hs_sem.at[i],
-            recv_sem=hr_sem.at[i],
-            device_id=device,
-            device_id_type=MESH,
+    for b in range(4):
+        halo.append(
+            pltpu.make_async_remote_copy(
+                src_ref=fgh_s.at[b],
+                dst_ref=ftab.at[pl.ds(ROWS + lands[b] * HALO, HALO)],
+                send_sem=hs_sem.at[b],
+                recv_sem=hr_sem.at[lands[b]],
+                device_id=sides[b],
+                device_id_type=MESH,
+            )
         )
-        copy.start()
-        halo.append(copy)
+    for b in (3, 1, 2, 0):
+        on_side(b, halo[b].start)
 
     for copy in weights_in:
         copy.wait()
@@ -94,7 +107,11 @@
     for copy in slots_in:
         copy.wait()
     slot_ids = lax.broadcasted_iota(I32, (SLOTS, ROWS), 0)
-    wanted = jnp.where((msk_v[...] > 0) | (slot_ids == 0), nbr_v[...], -1)
+    wanted = nbr_v[...]
+    block = wanted // HALO
+    moved = jnp.where(block == 2 + core, (3 - core) * HALO, jnp.where(block == 3 - core, (core - 1) * HALO, -HALO))
+    wanted = jnp.where(wanted < ROWS, wanted, wanted + moved)
+    wanted = jnp.where((msk_v[...] > 0) | (slot_ids == 0), wanted, -1)
     tile = 32
     for t in range(TABLE // tile):
         ids = lax.broadcasted_iota(I32, (tile, ROWS), 0) + t * tile
@@ -118,38 +135,48 @@
                 s_v[h, t : t + step, :] = s
                 tops[h] = jnp.maximum(tops[h], jnp.max(s.reshape(step // 8, 8, ROWS), axis=0))
 
-    products(0, ROWS)
-
-    for copy in halo:
-        copy.wait_recv()
-
-    @pl.when(lat == 0)
-    def _():
-        ftab[ROWS + 2 * HALO : ROWS + 3 * HALO, :] = jnp.zeros((HALO, D), BF16)
-
-    @pl.when(lat == 7)
-    def _():
-        ftab[ROWS + 3 * HALO : ROWS + 4 * HALO, :] = jnp.zeros((HALO, D), BF16)
-
-    others = ftab[ROWS:TABLE, :]
-    k_v[ROWS:TABLE, :] = dot(others, w_v[1]).astype(BF16)
-    v_v[ROWS:TABLE, :] = dot(others, w_v[2]).astype(BF16)
-    products(ROWS, TABLE)
-
-    for h in range(HEADS):
-        cols = slice(h * HEAD, (h + 1) * HEAD)
-        top = jnp.max(tops[h], axis=0, keepdims=True)
+    def softmax_start(h, lo, hi, top):
         total = jnp.zeros((8, ROWS), F32)
         inner = jnp.zeros((8, ROWS), F32)
-        for t in range(0, TABLE, step):
+        for t in range(lo, hi, step):
             e = jnp.exp((s_v[h, t : t + step, :] - top) * SCALE)
             s_v[h, t : t + step, :] = e
             total += jnp.sum(e.reshape(step // 8, 8, ROWS), axis=0)
             inner += jnp.sum((e * dp_v[h, t : t + step, :]).reshape(step // 8, 8, ROWS), axis=0)
-        inverse = 1.0 / jnp.sum(total, axis=0, keepdims=True)
-        inner = jnp.sum(inner, axis=0, keepdims=True) * inverse
+        return jnp.sum(total, axis=0, keepdims=True), jnp.sum(inner, axis=0, keepdims=True)
+
+    products(0, ROWS)
+
+    for b in range(4):
+        lo, hi = ROWS + b * HALO, ROWS + (b + 1) * HALO
+        if b == 3:
+            early = [jnp.max(tops[h], axis=0, keepdims=True) for h in range(HEADS)]
+            sums = [softmax_start(h, 0, lo, early[h]) for h in range(HEADS)]
+        on_side(b, halo[lands[b]].wait_recv)
+        if b in (1, 2):
+
+            @pl.when(lat == (0 if b == 1 else 7))
+            def _():
+                ftab[lo:hi, :] = jnp.zeros((HALO, D), BF16)
+
+        rows = ftab[lo:hi, :]
+        k_v[lo:hi, :] = dot(rows, w_v[1]).astype(BF16)
+        v_v[lo:hi, :] = dot(rows, w_v[2]).astype(BF16)
+        products(lo, hi)
+
+    last = TABLE - HALO
+    for h in range(HEADS):
+        cols = slice(h * HEAD, (h + 1) * HEAD)
+        top = jnp.max(tops[h], axis=0, keepdims=True)
+        fall = jnp.exp((early[h] - top) * SCALE)
+        total, inner = softmax_start(h, last, TABLE, top)
+        total += sums[h][0] * fall
+        inner += sums[h][1] * fall
+        inverse = 1.0 / total
+        inner *= inverse
+        fall *= inverse
         for t in range(0, TABLE, step):
-            p = s_v[h, t : t + step, :] * inverse
+            p = s_v[h, t : t + step, :] * (fall if t < last else inverse)
             p_v[h, t : t + step, :] = p.astype(BF16)
             ds_v[h, t : t + step, :] = (p * (dp_v[h, t : t + step, :] - inner) * SCALE).astype(BF16)
         gq_v[:, cols] = dot(ds_v[h], k_v[:, cols], TN).astype(BF16)
@@ -226,49 +253,51 @@
         gv_v[:, cols] = dot(p_v[h], cot_v[:, cols]).astype(BF16)
         if h >= 2:
             gk_v[:, cols] = dot(ds_v[h], q_v[:, cols]).astype(BF16)
+    plane_a = to_plane(0, core_a)
     dw_v[D + 256 : 2 * D, :] = dot(gk_v[:, 256:512], ftab[...], TN).astype(BF16)
     dw_v[2 * D : 3 * D, :] = dot(gv_v[...], ftab[...], TN).astype(BF16)
-    plane_a = to_plane(0, core_a)
     core_b = to_partner(1)
     fg_own[...] = (
         dot(gq_v[...], w_v[0], NT) + dot(gk_v[0:ROWS, :], w_v[1], NT) + dot(gv_v[0:ROWS, :], w_v[2], NT)
     )
     plane_b = to_plane(1, core_b)
 
-    for copy in halo:
-        copy.wait_send()
+    back = []
     for b in range(4):
+        back.append(
+            pltpu.make_async_remote_copy(
+                src_ref=fgh_s.at[b],
+                dst_ref=fgh_r.at[pl.ds(lands[b] * HALO, HALO)],
+                send_sem=rs_sem.at[b],
+                recv_sem=rr_sem.at[lands[b]],
+                device_id=sides[b],
+                device_id_type=MESH,
+            )
+        )
+    for b in (3, 1, 2, 0):
+        on_side(b, halo[b].wait_send)
         rows = slice(ROWS + b * HALO, ROWS + (b + 1) * HALO)
         fgh_s[b] = (dot(gk_v[rows, :], w_v[1], NT) + dot(gv_v[rows, :], w_v[2], NT)).astype(BF16)
     to_z(0, plane_a)
-    back = []
-    for i, (b, block, device) in enumerate(sides):
-        copy = pltpu.make_async_remote_copy(
-            src_ref=fgh_s.at[b],
-            dst_ref=fgh_r.at[pl.ds(block * HALO, HALO)],
-            send_sem=rs_sem.at[i],
-            recv_sem=rr_sem.at[i],
-            device_id=device,
-            device_id_type=MESH,
-        )
-        copy.start()
-        back.append(copy)
+    for b in (3, 1, 2, 0):
+        on_side(b, back[b].start)
     to_z(1, plane_b)
 
-    for copy in back:
-        copy.wait_recv()
+    for b in range(4):
+        on_side(lands[b], back[b].wait_recv)
+        on_side(b, back[b].wait_send)
 
     @pl.when(lat == 0)
     def _():
-        fgh_r[2 * HALO : 3 * HALO, :] = jnp.zeros((HALO, D), BF16)
+        fgh_r[1 * HALO : 2 * HALO, :] = jnp.zeros((HALO, D), BF16)
 
     @pl.when(lat == 7)
     def _():
-        fgh_r[3 * HALO : 4 * HALO, :] = jnp.zeros((HALO, D), BF16)
+        fgh_r[2 * HALO : 3 * HALO, :] = jnp.zeros((HALO, D), BF16)
 
     fg_out[...] = (fg_own[...] + dot(picked[...], fgh_r[...])).astype(BF16)
 
-    for copy in back + [core_a, core_b] + plane_a + plane_b:
+    for copy in [core_a, core_b] + plane_a + plane_b:
         copy.wait_send()
     zrecv[z] = zsend[z]
     for other in range(8):

time: 45.1 us -> 41.3 us (0.916)
  Pallas kernels: 42.1 us -> 38.2 us
    pallas_call x1, Pallas kernels: 42.1 us -> 38.2 us  [shards(): pl.pallas_call(kernel, out_shape=(jax.ShapeDtypeStruct((ROWS, D), BF16),...]
where the time goes in v3:
time: 41.3 us; the launch traced here: 41.2 us
  Pallas kernels  38.2 us (92%)
  local copies, waits for them, and re-layouts  2.28 us (6%)
  between operations  0.65 us (2%)
    pallas_call x1, Pallas kernels, shards(): pl.pallas_call(kernel, out_shape=(jax.ShapeDtypeStruct((ROWS, D), BF16),...  38.2 us
    unnamed x4, local copies, waits for them, and re-layouts  2.28 us

profile of v3, /device:TPU:1, one launch (start us, length us, event | category | flops | bytes accessed | tf_op | source)
XLA Modules:
  0.0 41.2 jit_solution(18269596914197741523)
XLA Ops:
  0.6 38.2 %mesh_attention_backward.1 = (bf16[256,512]{1,0:T(8,128)(2,1)}, f32[6,512]{1,0:T(8,128)}) custom-call(bf16[256,512]{1,0:T(8,128)(2,1)} %feat.1, bf16[256,512]{1,0:T(8,128)(2,1)} %cot.1, bf16[512,512]{1,0:T(8,128)(2,1)} %w_query.1, bf16[512,512]{1,0:T(8,128)(2,1)} %w_key.1, bf16[512,512]{1,0:T(8,128)(2,1)} %w_value.1, s32[16,256]{1,0:T(8,128)} %bitcast.2, ...), custom_call_target="tpu_custom_call" | custom-call | tf_op jit(solution)/shard_map/mesh_attention_backward/pallas_call | solution.py:326
  38.9 0.0 copy-start
  38.9 1.7 %copy.13 = bf16[256,512]{1,0:T(8,128)(2,1)} copy(bf16[256,512]{1,0:T(8,128)(2,1)} %get-tuple-element.4) | data formatting | bytes 524288
  40.5 0.0 copy-done
  40.6 0.6 %copy.14 = f32[6,512]{1,0:T(8,128)} copy(f32[6,512]{1,0:T(8,128)S(1)} %copy-done) | data formatting | bytes 24576
Async XLA Ops:
  38.9 1.7 %copy-start = (f32[6,512]{1,0:T(8,128)S(1)}, f32[6,512]{1,0:T(8,128)}, u32[]{:S(2)}) copy-start(f32[6,512]{1,0:T(8,128)} %get-tuple-element.5) | copy-start | bytes 36868

commit v4 on v3

--- a/solution.py
+++ b/solution.py
@@ -34,6 +34,7 @@
     picked, q_v, k_v, v_v, bias, s_v, dp_v, p_v, ds_v, gq_v, gk_v, gv_v, dw_v,
     part, crecv, acc1, precv, acc2, zsend, zrecv, fg_own, fgh_s, fgh_r,
     in_sem, hs_sem, hr_sem, cs_sem, cr_sem, ps_sem, pr_sem, zs_sem, zr_sem, rs_sem, rr_sem,
+    result, out_sem,
 ):
     lon, lat = lax.axis_index("lon"), lax.axis_index("lat")
     z, core = lon // 4, lon % 2
@@ -64,7 +65,10 @@
         copy.start()
         return copy
 
-    rows_in = [load(0, snd, snd_v), load(1, feat, ftab.at[pl.ds(0, ROWS)])]
+    rows_in = [load(0, snd, snd_v)]
+    for i in range(4):
+        quarter = pl.ds(i * 64, 64)
+        rows_in.append(load(9 + i, feat.at[quarter], ftab.at[quarter]))
     barrier = pltpu.get_barrier_semaphore()
     peers = [far, partner] + plane_peers + [(((z + d) % 8) * 4 + lon % 4, lat) for d in (4, 3, 5, 2, 6, 1, 7)]
     for peer in peers:
@@ -72,9 +76,6 @@
 
     for copy in rows_in:
         copy.wait()
-    weights_in = [load(2, w_query, w_v.at[0]), load(3, w_key, w_v.at[1]), load(4, w_value, w_v.at[2])]
-    slots_in = [load(5, nbr, nbr_v), load(6, msk, msk_v)]
-    rest_in = [load(7, cot, cot_v), load(8, perm, perm_v)]
     row_ids = lax.broadcasted_iota(I32, (ROWS, HALO), 0)
     below, above = snd_v[0:1, :], snd_v[1:2, :]
     lists = [jnp.where(core == 0, above, below), snd_v[2:3, :], snd_v[3:4, :], jnp.where(core == 0, below, above)]
@@ -98,6 +99,9 @@
     for b in (3, 1, 2, 0):
         on_side(b, halo[b].start)
 
+    weights_in = [load(2, w_query, w_v.at[0]), load(3, w_key, w_v.at[1]), load(4, w_value, w_v.at[2])]
+    slots_in = [load(5, nbr, nbr_v), load(6, msk, msk_v)]
+    rest_in = [load(7, cot, cot_v), load(8, perm, perm_v)]
     for copy in weights_in:
         copy.wait()
     own = ftab[0:ROWS, :]
@@ -257,10 +261,10 @@
     dw_v[D + 256 : 2 * D, :] = dot(gk_v[:, 256:512], ftab[...], TN).astype(BF16)
     dw_v[2 * D : 3 * D, :] = dot(gv_v[...], ftab[...], TN).astype(BF16)
     core_b = to_partner(1)
+    plane_b = to_plane(1, core_b)
     fg_own[...] = (
         dot(gq_v[...], w_v[0], NT) + dot(gk_v[0:ROWS, :], w_v[1], NT) + dot(gv_v[0:ROWS, :], w_v[2], NT)
     )
-    plane_b = to_plane(1, core_b)
 
     back = []
     for b in range(4):
@@ -283,9 +287,8 @@
         on_side(b, back[b].start)
     to_z(1, plane_b)
 
-    for b in range(4):
+    for b in range(3):
         on_side(lands[b], back[b].wait_recv)
-        on_side(b, back[b].wait_send)
 
     @pl.when(lat == 0)
     def _():
@@ -295,7 +298,7 @@
     def _():
         fgh_r[2 * HALO : 3 * HALO, :] = jnp.zeros((HALO, D), BF16)
 
-    fg_out[...] = (fg_own[...] + dot(picked[...], fgh_r[...])).astype(BF16)
+    fg_own[...] += dot(picked[:, 0 : 3 * HALO], fgh_r[0 : 3 * HALO, :])
 
     for copy in [core_a, core_b] + plane_a + plane_b:
         copy.wait_send()
@@ -314,6 +317,17 @@
     for other in range(1, 8):
         total += zrecv[other].astype(F32)
     dw_out[...] = jnp.concatenate([total[0:6, :], total[8:14, :]], axis=1)
+    for b in range(4):
+        on_side(b, back[b].wait_send)
+    back[3].wait_recv()
+    fg_copies = []
+    for i in range(2):
+        rows = slice(i * 128, (i + 1) * 128)
+        result[rows, :] = (fg_own[rows, :] + dot(picked[rows, 3 * HALO :], fgh_r[3 * HALO :, :])).astype(BF16)
+        fg_copies.append(pltpu.make_async_copy(result.at[pl.ds(i * 128, 128)], fg_out.at[pl.ds(i * 128, 128)], out_sem.at[i]))
+        fg_copies[i].start()
+    for copy in fg_copies:
+        copy.wait()
 
 
 def sorting():
@@ -321,13 +335,19 @@
     return (source[:, None] == np.arange(192)[None, :]).astype(np.float32)
 
 
+def handing_on(fg, dw, fg_out, dw_out):
+    fg_out[...] = fg[...]
+    dw_out[...] = dw[...]
+
+
 def shards(features, cotangent, w_query, w_key, w_value, neighbour, slot_mask, send_rows):
     whole = pl.BlockSpec(memory_space=VMEM)
-    return pl.pallas_call(
+    shapes = (jax.ShapeDtypeStruct((ROWS, D), BF16), jax.ShapeDtypeStruct((6, D), F32))
+    results = pl.pallas_call(
         kernel,
-        out_shape=(jax.ShapeDtypeStruct((ROWS, D), BF16), jax.ShapeDtypeStruct((6, D), F32)),
+        out_shape=shapes,
         in_specs=[pl.BlockSpec(memory_space=pl.ANY)] * 9,
-        out_specs=(whole, whole),
+        out_specs=(pl.BlockSpec(memory_space=pl.ANY), whole),
         scratch_shapes=[
             VMEM((TABLE, D), BF16), VMEM((ROWS, D), BF16), VMEM((3, D, D), BF16), VMEM((SLOTS, ROWS), I32),
             VMEM((SLOTS, ROWS), I32), VMEM((4, HALO), I32), VMEM((192, 192), BF16),
@@ -338,8 +358,9 @@
             VMEM((2, 2, 16, 48, 256), BF16), VMEM((2, 16, 48, 256), BF16), VMEM((2, 16, 48, 256), BF16),
             VMEM((2, 15, 48, 256), BF16), VMEM((2, 32, D), F32), VMEM((8, 16, 256), BF16), VMEM((8, 16, 256), BF16),
             VMEM((ROWS, D), F32), VMEM((4, HALO, D), BF16), VMEM((4 * HALO, D), BF16),
-            DMA((9,)), DMA((4,)), DMA((4,)), DMA((2,)), DMA((2,)), DMA((2, 15)), DMA((2, 15)),
+            DMA((13,)), DMA((4,)), DMA((4,)), DMA((2,)), DMA((2,)), DMA((2, 15)), DMA((2, 15)),
             DMA((8,)), DMA((8,)), DMA((4,)), DMA((4,)),
+            VMEM((ROWS, D), BF16), DMA((2,)),
         ],
         compiler_params=pltpu.CompilerParams(
             collective_id=0, has_side_effects=True, vmem_limit_bytes=60 * 1024 * 1024
@@ -349,6 +370,14 @@
         features, cotangent, w_query, w_key, w_value, neighbour.T, slot_mask.T, send_rows,
         jnp.asarray(sorting(), BF16),
     )
+    return pl.pallas_call(
+        handing_on,
+        out_shape=shapes,
+        in_specs=[whole] * 2,
+        out_specs=(whole,) * 2,
+        compiler_params=pltpu.CompilerParams(vmem_limit_bytes=60 * 1024 * 1024),
+        name="handing_on",
+    )(*results)
 
 
 def solution(mesh):

time: 41.3 us -> 41.2 us (level)
  local copies, waits for them, and re-layouts: 2.28 us -> 0 us
  Pallas kernels: 38.2 us -> 40.3 us
    unnamed x4 -> x0, local copies, waits for them, and re-layouts: 2.28 us -> none
    pallas_call x1 -> x2, Pallas kernels: 38.2 us -> 40.3 us  [the longest x1 38.7 us: shards(): pl.pallas_call(kernel, out_shape=shapes, in_specs=[pl.BlockSpec(memory_sp...]
where the time goes in v4:
time: 41.2 us; the launch traced here: 41 us
  Pallas kernels  40.3 us (98%)
  between operations  0.64 us (2%)
    pallas_call x1, Pallas kernels, shards(): pl.pallas_call(kernel, out_shape=shapes, in_specs=[pl.BlockSpec(memory_sp...  38.7 us
    pallas_call x1, Pallas kernels, shards(): pl.pallas_call(handing_on, out_shape=shapes, in_specs=[whole] * 2, out_sp...  1.68 us

profile of v4, /device:TPU:1, one launch (start us, length us, event | category | flops | bytes accessed | tf_op | source)
XLA Modules:
  0.0 41.0 jit_solution(8740922638202007535)
XLA Ops:
  0.6 38.7 %mesh_attention_backward.1 = (bf16[256,512]{1,0:T(8,128)(2,1)}, f32[6,512]{1,0:T(8,128)}) custom-call(bf16[256,512]{1,0:T(8,128)(2,1)} %feat.1, bf16[256,512]{1,0:T(8,128)(2,1)} %cot.1, bf16[512,512]{1,0:T(8,128)(2,1)} %w_query.1, bf16[512,512]{1,0:T(8,128)(2,1)} %w_key.1, bf16[512,512]{1,0:T(8,128)(2,1)} %w_value.1, s32[16,256]{1,0:T(8,128)} %bitcast.2, ...), custom_call_target="tpu_custom_call" | custom-call | tf_op jit(solution)/shard_map/mesh_attention_backward/pallas_call | solution.py:346
  39.3 1.7 %handing_on.1 = (bf16[256,512]{1,0:T(8,128)(2,1)}, f32[6,512]{1,0:T(8,128)}) custom-call(bf16[256,512]{1,0:T(8,128)(2,1)} %get-tuple-element.4.fg, f32[6,512]{1,0:T(8,128)} %get-tuple-element.5.dw), custom_call_target="tpu_custom_call" | custom-call | tf_op jit(solution)/shard_map/handing_on/pallas_call | solution.py:373

commit v5 on v3

--- a/solution.py
+++ b/solution.py
@@ -257,10 +257,10 @@
     dw_v[D + 256 : 2 * D, :] = dot(gk_v[:, 256:512], ftab[...], TN).astype(BF16)
     dw_v[2 * D : 3 * D, :] = dot(gv_v[...], ftab[...], TN).astype(BF16)
     core_b = to_partner(1)
+    plane_b = to_plane(1, core_b)
     fg_own[...] = (
         dot(gq_v[...], w_v[0], NT) + dot(gk_v[0:ROWS, :], w_v[1], NT) + dot(gv_v[0:ROWS, :], w_v[2], NT)
     )
-    plane_b = to_plane(1, core_b)
 
     back = []
     for b in range(4):
@@ -278,8 +278,10 @@
         on_side(b, halo[b].wait_send)
         rows = slice(ROWS + b * HALO, ROWS + (b + 1) * HALO)
         fgh_s[b] = (dot(gk_v[rows, :], w_v[1], NT) + dot(gv_v[rows, :], w_v[2], NT)).astype(BF16)
+    for b in (1, 2, 0):
+        on_side(b, back[b].start)
     to_z(0, plane_a)
-    for b in (3, 1, 2, 0):
+    for b in (3,):
         on_side(b, back[b].start)
     to_z(1, plane_b)
 

time: 41.3 us -> 41.3 us (level)
  no operation moved by 1% of the time
where the time goes in v5:
time: 41.3 us; the launch traced here: 41.2 us
  Pallas kernels  38.3 us (93%)
  local copies, waits for them, and re-layouts  2.28 us (6%)
  between operations  0.65 us (2%)
    pallas_call x1, Pallas kernels, shards(): pl.pallas_call(kernel, out_shape=(jax.ShapeDtypeStruct((ROWS, D), BF16),...  38.3 us
    unnamed x4, local copies, waits for them, and re-layouts  2.28 us

profile of v5, /device:TPU:1, one launch (start us, length us, event | category | flops | bytes accessed | tf_op | source)
XLA Modules:
  0.0 41.2 jit_solution(12257483161115632314)
XLA Ops:
  0.6 38.3 %mesh_attention_backward.1 = (bf16[256,512]{1,0:T(8,128)(2,1)}, f32[6,512]{1,0:T(8,128)}) custom-call(bf16[256,512]{1,0:T(8,128)(2,1)} %feat.1, bf16[256,512]{1,0:T(8,128)(2,1)} %cot.1, bf16[512,512]{1,0:T(8,128)(2,1)} %w_query.1, bf16[512,512]{1,0:T(8,128)(2,1)} %w_key.1, bf16[512,512]{1,0:T(8,128)(2,1)} %w_value.1, s32[16,256]{1,0:T(8,128)} %bitcast.2, ...), custom_call_target="tpu_custom_call" | custom-call | tf_op jit(solution)/shard_map/mesh_attention_backward/pallas_call | solution.py:328
  38.9 0.0 copy-start
  38.9 1.7 %copy.13 = bf16[256,512]{1,0:T(8,128)(2,1)} copy(bf16[256,512]{1,0:T(8,128)(2,1)} %get-tuple-element.4) | data formatting | bytes 524288
  40.6 0.0 copy-done
  40.6 0.6 %copy.14 = f32[6,512]{1,0:T(8,128)} copy(f32[6,512]{1,0:T(8,128)S(1)} %copy-done) | data formatting | bytes 24576
Async XLA Ops:
  38.9 1.7 %copy-start = (f32[6,512]{1,0:T(8,128)S(1)}, f32[6,512]{1,0:T(8,128)}, u32[]{:S(2)}) copy-start(f32[6,512]{1,0:T(8,128)} %get-tuple-element.5) | copy-start | bytes 36868
